TPU v7x, 32 devices: a whole 2x2x4 slice. The times are simulated.
32 devices in a mesh: agent: 4 (over y, x), tile: 8 (over z, core).
Axes of the slice: x: 2, y: 2, z: 4, core: 2. Of those that a mesh axis runs over, the one named last changes fastest.
Arguments:
- feats: bfloat16 [32, 32, 24, 256], P('agent', 'tile'), may hold values from -18 to 18
- types: int32 [32], replicated, may hold values from 0 to 1
- valid: int32 [32], replicated, may hold values 0 or 1
- offsets: int32 [32, 2], replicated, may hold values from -2 to 2
- w_qkv: bfloat16 [2, 256, 768], replicated, may hold values from -0.375 to 0.375
- w_out: bfloat16 [2, 256, 256], replicated, may hold values from -0.375 to 0.375
- d_out: bfloat16 [32, 32, 24, 256], P('agent', 'tile'), may hold values from -6 to 6
Outputs:
- d_feats: bfloat16 [32, 32, 24, 256], P('agent', 'tile')
- g_qkv: float32 [2, 256, 768], P(None, 'tile')
- g_out: float32 [2, 256, 256], P(None, 'tile')
All inputs are finite; a program needn't handle non-finite values.
Results may differ from a plain program's by a relative error of at most 0.012.
The roundings to bfloat16 on the way count: a program that leaves them out, or rounds other values in their place, can miss the bound.
Values may be sent and summed in bfloat16 or wider, within the bound.
A program may use at most 128 MiB of HBM per device.

v0:
```python
import math

import jax
import jax.numpy as jnp
from jax import lax
from jax.sharding import PartitionSpec as P

HEADS = 8
MAXOFF = 2


def with_halo(cells, sides, width):
    for axis, dim in sides:
        count = lax.axis_size(axis)
        ends = count - 1
        head = lax.slice_in_dim(cells, 0, width, axis=dim)
        tail = lax.slice_in_dim(cells, cells.shape[dim] - width, cells.shape[dim], axis=dim)
        cells = jnp.concatenate(
            [
                lax.ppermute(tail, axis, [(i, (i + 1) % count) for i in range(ends)]),
                cells,
                lax.ppermute(head, axis, [((i + 1) % count, i) for i in range(ends)]),
            ],
            axis=dim,
        )
    return cells


def relocate(rimmed, offsets, direction):
    padded = jnp.pad(rimmed, ((0, 0), (0, 0), (MAXOFF, MAXOFF), (0, 0)))
    row_count = rimmed.shape[1] - 2 * MAXOFF
    col_count = rimmed.shape[2]

    def pick_one(plane, offset):
        row_start = MAXOFF + direction * offset[0]
        col_start = MAXOFF + direction * offset[1]
        return lax.dynamic_slice(
            plane, (row_start, col_start, jnp.int32(0)), (row_count, col_count, plane.shape[2])
        )

    return jax.vmap(pick_one)(padded, offsets)


def body(feats, types, valid, offsets, w_qkv, w_out, d_out):
    f32 = jnp.float32
    bf16 = jnp.bfloat16
    highest = lax.Precision.HIGHEST
    own_count, row_count, col_count, channels = feats.shape
    agents = own_count * lax.axis_size("agent")
    first_agent = lax.axis_index("agent") * own_count
    own_offsets = lax.dynamic_slice_in_dim(offsets, first_agent, own_count, 0)
    rimmed = with_halo(feats, (("tile", 1),), MAXOFF)
    warped = relocate(rimmed, own_offsets, 1)
    cell_count = row_count * col_count
    head_size = channels // HEADS
    score_scale = head_size ** (-0.5)
    all_hot = (types[:, None] == jnp.arange(2)[None, :]).astype(bf16)
    flat_feats = warped.reshape(own_count, cell_count, channels)
    flat_grads = d_out.reshape(own_count, cell_count, channels)
    all_feats, all_grads = (
        lax.all_to_all(flat_feats, "agent", split_axis=1, concat_axis=0, tiled=True),
        lax.all_to_all(flat_grads, "agent", split_axis=1, concat_axis=0, tiled=True),
    )
    part_cells = all_feats.shape[1]
    wqkv_all = jnp.take(w_qkv, types, axis=0)
    wout_all = jnp.take(w_out, types, axis=0)
    qkv = jnp.einsum("bgc,bce->bge", all_feats, wqkv_all, preferred_element_type=f32).astype(bf16)
    query_heads = qkv[..., :channels].reshape(agents, part_cells, HEADS, head_size)
    key_heads = qkv[..., channels : 2 * channels].reshape(agents, part_cells, HEADS, head_size)
    value_heads = qkv[..., 2 * channels :].reshape(agents, part_cells, HEADS, head_size)
    scores = (
        jnp.einsum("aghd,bghd->ghab", query_heads, key_heads, preferred_element_type=f32)
        * score_scale
    )
    agent_ids = jnp.arange(agents)
    allowed = (valid[None, :] == 1) | (agent_ids[:, None] == agent_ids[None, :])
    raised = jnp.where(allowed, jnp.exp(scores), f32(0.0))
    attn_prob = raised / jnp.sum(raised, axis=-1, keepdims=True)
    prob_low = attn_prob.astype(bf16)
    attended = (
        jnp.einsum("ghab,bghd->aghd", prob_low, value_heads, preferred_element_type=f32)
        .astype(bf16)
        .reshape(agents, part_cells, channels)
    )
    d_attended = jnp.einsum("age,ace->agc", all_grads, wout_all, preferred_element_type=f32).astype(
        bf16
    )
    attended_typed = all_hot[:, :, None, None] * attended[:, None]
    raw_out = jnp.einsum("atgc,age->tce", attended_typed, all_grads, preferred_element_type=f32)
    attended_heads = d_attended.reshape(agents, part_cells, HEADS, head_size)
    prob_grad = jnp.einsum(
        "aghd,bghd->ghab", attended_heads, value_heads, preferred_element_type=f32
    )
    score_grad = (
        attn_prob
        * (prob_grad - jnp.sum(attn_prob * prob_grad, axis=-1, keepdims=True))
        * score_scale
    ).astype(bf16)
    d_query = (
        jnp.einsum("ghab,bghd->aghd", score_grad, key_heads, preferred_element_type=f32)
        .astype(bf16)
        .reshape(agents, part_cells, channels)
    )
    groups_n = agents // own_count
    grad_blocks = score_grad.reshape(part_cells, HEADS, groups_n, own_count, agents)
    prob_blocks = prob_low.reshape(part_cells, HEADS, groups_n, own_count, agents)
    query_blocks = query_heads.reshape(groups_n, own_count, part_cells, HEADS, head_size)
    dattn_blocks = attended_heads.reshape(groups_n, own_count, part_cells, HEADS, head_size)
    key_parts = jnp.einsum(
        "ghnyb,nyghd->nbghd", grad_blocks, query_blocks, preferred_element_type=f32
    ).astype(bf16)
    value_parts = jnp.einsum(
        "ghnyb,nyghd->nbghd", prob_blocks, dattn_blocks, preferred_element_type=f32
    ).astype(bf16)
    key_sum = jnp.sum(key_parts.astype(f32), axis=0).reshape(agents, part_cells, channels)
    value_sum = jnp.sum(value_parts.astype(f32), axis=0).reshape(agents, part_cells, channels)
    d_qkv = jnp.concatenate([d_query.astype(f32), key_sum, value_sum], axis=-1)
    d_part = jnp.einsum("bge,bce->bgc", d_qkv, wqkv_all.astype(f32), precision=highest).astype(bf16)
    returned = lax.all_to_all(d_part, "agent", split_axis=0, concat_axis=1, tiled=True)
    d_warped = returned.reshape(own_count, row_count, col_count, channels)
    type_wide = all_hot.astype(f32)
    raw_qkv = jnp.einsum(
        "bt,bgc,bge->tce", type_wide, all_feats.astype(f32), d_qkv, precision=highest
    )
    rimmed_grad = with_halo(d_warped, (("tile", 1),), MAXOFF)
    d_feats = relocate(rimmed_grad, own_offsets, -1)
    norm_limit = math.sqrt(8.0 * channels * channels)
    part_qkv, part_out = (
        lax.psum_scatter(raw_qkv, "tile", scatter_dimension=1, tiled=True),
        lax.psum_scatter(raw_out, "tile", scatter_dimension=1, tiled=True),
    )
    share_qkv, share_out = (
        lax.psum(part_qkv.astype(jnp.bfloat16), "agent").astype(jnp.float32),
        lax.psum(part_out.astype(jnp.bfloat16), "agent").astype(jnp.float32),
    )
    local_squares = jnp.sum(share_qkv * share_qkv) + jnp.sum(share_out * share_out)
    square_sum = lax.psum(local_squares, "tile")
    factor = norm_limit / jnp.maximum(jnp.sqrt(square_sum), norm_limit)
    return (d_feats, share_qkv * factor, share_out * factor)


def solution(mesh):
    placed = (
        P("agent", "tile", None, None),
        P(),
        P(),
        P(),
        P(),
        P(),
        P("agent", "tile", None, None),
    )
    return jax.shard_map(
        body,
        mesh=mesh,
        in_specs=placed,
        out_specs=(P("agent", "tile", None, None), P(None, "tile", None), P(None, "tile", None)),
        check_vma=False,
    )
```

profile of v0, /device:TPU:0, one launch (start us, length us, event | category | flops | bytes accessed | tf_op | source)
XLA Modules:
  0.0 316.0 jit_solution(18103586326757427185)
XLA Ops:
  10.1 5.2 %all-to-all-start.1 = ((bf16[8,96,256]{2,0,1:T(8,128)(2,1)}), bf16[8,96,256]{2,0,1:T(8,128)(2,1)S(1)}, u32[]{:S(2)}, u32[]{:S(2)}) async-start(bf16[8,96,256]{2,0,1:T(8,128)(2,1)} %bitcast.6), calls=%async_computation.1 | async-start | bytes 786432 | tf_op jit(solution)/shard_map/all_to_all | solution.py:62
  20.8 2.8 gather_fusion.1
  23.6 6.6 %gather_fusion = bf16[32,256,768]{2,1,0:T(8,128)(2,1)} fusion(bf16[2,256,768]{2,1,0:T(8,128)(2,1)S(1)} %copy-done, s32[1024]{0:T(1024)S(1)} %pad_clamp_fusion), kind=kCustom, calls=%fused_computation | custom fusion | bytes 25165952 | tf_op jit(solution)/shard_map/jit(_take)/gather | solution.py:65
  30.3 2.5 gather_fusion.2
  32.7 4.0 %all-to-all-start = ((bf16[8,96,256]{2,0,1:T(8,128)(2,1)}), bf16[8,96,256]{2,0,1:T(8,128)(2,1)S(1)}, u32[]{:S(2)}, u32[]{:S(2)}) async-start(bf16[8,96,256]{2,0,1:T(8,128)(2,1)} %bitcast.1), calls=%async_computation | async-start | bytes 786432 | tf_op jit(solution)/shard_map/all_to_all | solution.py:61
  37.6 3.5 %fusion.33 = bf16[32,24,256]{2,1,0:T(8,128)(2,1)S(1)} fusion(bf16[32,24,256]{2,1,0:T(8,128)(2,1)S(1)} %bitcast.80, bf16[32,256,256]{2,1,0:T(8,128)(2,1)} %gather_fusion.1, pred[32]{0:T(512)(128)(4,1)S(1)} %compare_and_fusion), kind=kOutput, calls=%fused_computation.43 | convolution fusion | flops 102957056 | bytes 4980768 | tf_op jit(solution)/shard_map/age,ace->agc/dot_general | solution.py:85
  44.7 6.7 %fusion.25 = bf16[32,24,768]{2,1,0:T(8,128)(2,1)S(1)} fusion(bf16[32,24,256]{2,1,0:T(8,128)(2,1)S(1)} %bitcast.77, bf16[32,256,768]{2,1,0:T(8,128)(2,1)} %gather_fusion, pred[32]{0:T(512)(128)(4,1)S(1)} %compare_and_fusion), kind=kOutput, calls=%fused_computation.38 | convolution fusion | flops 308871168 | bytes 14155808 | tf_op jit(solution)/shard_map/bgc,bce->bge/dot_general | solution.py:67
  57.9 3.8 %fusion.10 = (f32[24,8,32]{2,1,0:T(8,128)S(1)}, f32[24,8,32,32]{2,3,1,0:T(8,128)S(1)}) fusion(pred[32,32]{0,1:T(8,128)(4,1)S(1)} %fusion.48, bf16[32,24,8,32]{0,3,2,1:T(8,128)(2,1)S(1)} %bitcast.75, bf16[32,24,8,32]{3,2,1,0:T(8,128)(2,1)} %reshape.74), kind=kOutput, calls=%fused_computation.22 | convolution fusion | flops 13166592 | bytes 1598464 | tf_op jit(solution)/shard_map/aghd,bghd->ghab/dot_general | solution.py:72
  65.9 3.3 %convolution_convert_fusion = bf16[24,8,32,32]{3,2,1,0:T(8,128)(2,1)} fusion(bf16[32,24,8,32]{0,3,2,1:T(8,128)(2,1)} %bitcast.64, bf16[24,8,32,32]{2,3,1,0:T(8,128)(2,1)S(1)} %fusion.66), kind=kOutput, calls=%fused_computation.26 | convolution fusion | flops 12779520 | bytes 1179648 | tf_op jit(solution)/shard_map/ghab,bghd->aghd/dot_general | solution.py:81
  69.2 2.9 fusion.21
  72.1 8.3 %fusion.15 = f32[24,8,32,32]{3,2,1,0:T(8,128)} fusion(bf16[32,24,8,32]{0,3,2,1:T(8,128)(2,1)S(1)} %bitcast.76, f32[24,8,32,32]{2,3,1,0:T(8,128)} %fusion.21, f32[24,8,32,32]{2,3,1,0:T(8,128)} %copy-done.6, f32[24,8,32]{2,1,0:T(8,128)S(1)} %get-tuple-element.21, pred[32,32]{0,1:T(8,128)(4,1)S(1)} %fusion.48), kind=kOutput, calls=%fused_computation.28 | convolution fusion | flops 15144991 | bytes 2778112 | tf_op jit(solution)/shard_map/ghab,bghd->aghd/dot_general | solution.py:100
  80.4 7.8 %multiply_convert_fusion = bf16[24,8,32,32]{2,3,1,0:T(8,128)(2,1)} fusion(f32[24,8,32,32]{2,3,1,0:T(8,128)} %fusion.21, f32[24,8,32]{2,1,0:T(8,128)S(1)} %get-tuple-element.21, f32[24,8,32,32]{2,3,1,0:T(8,128)} %copy-done.6, pred[32,32]{0,1:T(8,128)(4,1)S(1)} %fusion.48), kind=kOutput, calls=%fused_computation.15 | output fusion | flops 2168863 | bytes 1991680 | tf_op jit(solution)/shard_map/sub | solution.py:96
  88.2 4.5 %convert_reduce_fusion = f32[24,8,32,32]{3,2,1,0:T(8,128)} fusion(bf16[4,8,24,8,32]{4,3,2,1,0:T(8,128)(2,1)S(1)} %copy-done.10, bf16[24,8,32,32]{3,2,1,0:T(8,128)(2,1)S(1)} %copy-done.9), kind=kOutput, calls=%fused_computation.7 | convolution fusion | flops 14745600 | bytes 1572864 | tf_op jit(solution)/shard_map/ghnyb,nyghd->nbghd/dot_general | solution.py:112
  92.7 2.5 copy.95
  98.4 5.4 %convert_reduce_fusion.1 = f32[24,8,32,32]{3,2,1,0:T(8,128)} fusion(bf16[4,8,24,8,32]{4,3,2,1,0:T(8,128)(2,1)} %reshape_reshape.6, bf16[24,8,32,32]{3,2,1,0:T(8,128)(2,1)S(1)} %copy.71), kind=kOutput, calls=%fused_computation.8 | convolution fusion | flops 14745600 | bytes 1572864 | tf_op jit(solution)/shard_map/ghnyb,nyghd->nbghd/dot_general | solution.py:109
  109.4 13.3 %fusion.16 = f32[32,768,256]{2,1,0:T(8,128)} fusion(bf16[32,24,256]{2,1,0:T(8,128)(2,1)S(1)} %bitcast.78, f32[32,24,256]{2,1,0:T(8,128)S(1)} %copy.95, f32[32,24,256]{2,1,0:T(8,128)S(1)} %copy.94, f32[32,24,256]{2,1,0:T(8,128)S(1)} %copy.79), kind=kOutput, calls=%fused_computation.29 | convolution fusion | flops 1813118976 | bytes 27918336 | tf_op jit(solution)/shard_map/bt,bgc,bge->tce/dot_general | solution.py:122
  122.7 38.8 %fusion.26 = f32[2,256,768]{1,0,2:T(2,128)S(1)} fusion(f32[32,768,256]{2,1,0:T(8,128)} %fusion.16, s32[32]{0:T(128)S(1)} %copy-done.17), kind=kOutput, calls=%fused_computation.39 | convolution fusion | flops 150995008 | bytes 26738816 | tf_op jit(solution)/shard_map/bt,bgc,bge->tce/dot_general | solution.py:122
  161.6 2.5 copy.82
  164.1 63.0 %all-reduce.7 = bf16[2,256,768]{2,0,1:T(2,128)(2,1)S(1)} all-reduce(f32[2,256,768]{2,0,1:T(2,128)} %copy.82), channel_id=2, replica_groups=mesh['agent'=4,'tile'=8] {'tile'}, use_global_device_ids=true, to_apply=%region_4.5.clone | all-reduce | flops 393216 | bytes 2359296
  230.3 12.5 %fusion.29 = bf16[32,24,256]{2,1,0:T(8,128)(2,1)S(1)} fusion(bf16[32,256,768]{2,1,0:T(8,128)(2,1)} %gather_fusion, pred[32]{0:T(512)(128)(4,1)S(1)} %compare_and_fusion, f32[32,24,256]{2,1,0:T(8,128)S(1)} %copy.95, f32[32,24,256]{2,1,0:T(8,128)S(1)} %copy.94, f32[32,24,256]{2,1,0:T(8,128)S(1)} %copy-done.8), kind=kOutput, calls=%fused_computation.40 | convolution fusion | flops 1819607040 | bytes 15335456 | tf_op jit(solution)/shard_map/bge,bce->bgc/dot_general | solution.py:118
  242.9 10.1 %all_to_all.51 = bf16[32,24,256]{2,1,0:T(8,128)(2,1)S(1)} all-to-all(bf16[32,24,256]{2,1,0:T(8,128)(2,1)S(1)} %fusion.29), channel_id=1, replica_groups=mesh['agent'=4,'tile'=8] {'agent'}, dimensions={0} | all-to-all | bytes 786432 | tf_op jit(solution)/shard_map/all_to_all | solution.py:119
  255.7 13.9 %all-reduce.6.cloned.1.call-done = bf16[2,32,768]{2,0,1:T(2,128)(2,1)} async-done(((bf16[2,32,768]{2,0,1:T(2,128)(2,1)}), bf16[2,32,768]{2,0,1:T(2,128)(2,1)}) %all-reduce.6.cloned.1.call-update) | async-done | bytes 98320 | tf_op jit(solution)/shard_map/psum | solution.py:133
  274.1 15.3 %psum.22 = bf16[2,32,256]{2,1,0:T(8,128)(2,1)S(1)} all-reduce(bf16[2,32,256]{2,1,0:T(8,128)(2,1)S(1)} %convert_element_type.97), channel_id=1, replica_groups=mesh['agent'=4,'tile'=8] {'agent'}, use_global_device_ids=true, to_apply=%region_8.9 | all-reduce | flops 16384 | bytes 65536 | tf_op jit(solution)/shard_map/psum | solution.py:134
  292.2 14.1 %psum.23 = f32[]{:T(128)} all-reduce(f32[]{:T(128)S(6)} %add.89), channel_id=1, replica_groups=mesh['agent'=4,'tile'=8] {'tile'}, use_global_device_ids=true, to_apply=%region_10.11 | all-reduce | flops 1 | bytes 8 | tf_op jit(solution)/shard_map/psum | solution.py:137
  (96 shorter events, 43.9 us)
Async XLA Ops:
  8.0 15.6 %copy-start = (bf16[2,256,768]{2,1,0:T(8,128)(2,1)S(1)}, bf16[2,256,768]{2,1,0:T(8,128)(2,1)}, u32[]{:S(2)}) copy-start(bf16[2,256,768]{2,1,0:T(8,128)(2,1)} %param.11) | copy-start | bytes 2359300
  8.0 11.3 %copy-start.19 = (u32[32]{0:T(128)S(1)}, u32[32]{0:T(128)}, u32[]{:S(2)}) copy-start(u32[32]{0:T(128)} %constant.122) | copy-start | bytes 388
  8.0 11.3 %copy-start.17 = (s32[32]{0:T(128)S(1)}, s32[32]{0:T(128)}, u32[]{:S(2)}) copy-start(s32[32]{0:T(128)} %param.8) | copy-start | bytes 388
  8.0 12.6 %copy-start.18 = (s32[32]{0:T(128)S(1)}, s32[32]{0:T(128)}, u32[]{:S(2)}) copy-start(s32[32]{0:T(128)} %param.9) | copy-start | bytes 388
  8.0 12.6 %copy-start.16 = (s32[32,2]{0,1:T(2,128)S(1)}, s32[32,2]{0,1:T(2,128)}, u32[]{:S(2)}) copy-start(s32[32,2]{0,1:T(2,128)} %param.10) | copy-start | bytes 772
  8.1 12.8 %copy-start.2 = (bf16[2,256,256]{2,1,0:T(8,128)(2,1)S(1)}, bf16[2,256,256]{2,1,0:T(8,128)(2,1)}, u32[]{:S(2)}) copy-start(bf16[2,256,256]{2,1,0:T(8,128)(2,1)} %param.12) | copy-start | bytes 786436
  10.1 22.6 %all-to-all-start.1 = ((bf16[8,96,256]{2,0,1:T(8,128)(2,1)}), bf16[8,96,256]{2,0,1:T(8,128)(2,1)S(1)}, u32[]{:S(2)}, u32[]{:S(2)}) async-start(bf16[8,96,256]{2,0,1:T(8,128)(2,1)} %bitcast.6), calls=%async_computation.1 | async-start | bytes 786432 | tf_op jit(solution)/shard_map/all_to_all | solution.py:62
  16.5 13.7 %collective-permute-start = (bf16[8,2,24,256]{3,0,2,1:T(8,128)(2,1)S(1)}, bf16[8,2,24,256]{3,0,2,1:T(8,128)(2,1)S(1)}, u32[]{:S(2)}, u32[]{:S(2)}) collective-permute-start(bf16[8,2,24,256]{3,0,2,1:T(8,128)(2,1)S(1)} %get-tuple-element.17), channel_id=1, source_target_pairs={{0,1},{1,2},{2,3},{3,4},{4,5},{5,6},{6,7},{8,9},{9,10},{10,11},{11... | collective-permute-start | bytes 589832 | tf_op jit(solution)/shard_map/ppermute | solution.py:20
  18.0 12.2 %collective-permute-start.1 = (bf16[8,2,24,256]{3,0,2,1:T(8,128)(2,1)S(1)}, bf16[8,2,24,256]{3,0,2,1:T(8,128)(2,1)S(1)}, u32[]{:S(2)}, u32[]{:S(2)}) collective-permute-start(bf16[8,2,24,256]{3,0,2,1:T(8,128)(2,1)S(1)} %get-tuple-element.18), channel_id=1, source_target_pairs={{1,0},{2,1},{3,2},{4,3},{5,4},{6,5},{7,6},{9,8},{10,9},{11,10},{12... | collective-permute-start | bytes 589832 | tf_op jit(solution)/shard_map/ppermute | solution.py:22
  32.7 11.9 %all-to-all-start = ((bf16[8,96,256]{2,0,1:T(8,128)(2,1)}), bf16[8,96,256]{2,0,1:T(8,128)(2,1)S(1)}, u32[]{:S(2)}, u32[]{:S(2)}) async-start(bf16[8,96,256]{2,0,1:T(8,128)(2,1)} %bitcast.1), calls=%async_computation | async-start | bytes 786432 | tf_op jit(solution)/shard_map/all_to_all | solution.py:61
  36.7 232.9 %all-reduce.6.cloned.1.call-start = ((), (), s32[]{:S(2)}) async-start(), calls=%async_computation.4 | async-start | bytes 196608 | tf_op jit(solution)/shard_map/psum | solution.py:133
  57.9 3.8 %copy-start.11 = (bf16[32,24,256]{0,2,1:T(8,128)(2,1)}, bf16[32,24,256]{0,2,1:T(8,128)(2,1)S(1)}, u32[]{:S(2)}) copy-start(bf16[32,24,256]{0,2,1:T(8,128)(2,1)S(1)} %copy.96) | copy-start | bytes 1179652
  65.8 3.3 %copy-start.3 = (bf16[32,24,256]{0,2,1:T(8,128)(2,1)S(1)}, bf16[32,24,256]{0,2,1:T(8,128)(2,1)}, u32[]{:S(2)}) copy-start(bf16[32,24,256]{0,2,1:T(8,128)(2,1)} %copy.97) | copy-start | bytes 1179652
  65.9 3.3 %copy-start.4 = (bf16[32,24,8,32]{3,2,1,0:T(8,128)(2,1)S(1)}, bf16[32,24,8,32]{3,2,1,0:T(8,128)(2,1)}, u32[]{:S(2)}) copy-start(bf16[32,24,8,32]{3,2,1,0:T(8,128)(2,1)} %reshape.76) | copy-start | bytes 1179652
  69.2 2.9 copy-start.12
  80.4 7.8 %copy-start.9 = (bf16[24,8,32,32]{3,2,1,0:T(8,128)(2,1)S(1)}, bf16[24,8,32,32]{3,2,1,0:T(8,128)(2,1)}, u32[]{:S(2)}) copy-start(bf16[24,8,32,32]{3,2,1,0:T(8,128)(2,1)} %copy.75) | copy-start | bytes 1179652
  80.4 7.8 %copy-start.10 = (bf16[4,8,24,8,32]{4,3,2,1,0:T(8,128)(2,1)S(1)}, bf16[4,8,24,8,32]{4,3,2,1,0:T(8,128)(2,1)}, u32[]{:S(2)}) copy-start(bf16[4,8,24,8,32]{4,3,2,1,0:T(8,128)(2,1)} %reshape_reshape.7) | copy-start | bytes 1179652
  92.7 2.5 copy-start.5
  161.6 66.4 %copy-start.14 = (bf16[4,8,24,256]{3,2,1,0:T(8,128)(2,1)S(1)}, bf16[4,8,24,256]{3,2,1,0:T(8,128)(2,1)}, u32[]{:S(2)}) copy-start(bf16[4,8,24,256]{3,2,1,0:T(8,128)(2,1)} %copy-done.13) | copy-start | bytes 1179652
  227.9 45.3 %reduce-scatter.2.cloned.1.call-start = ((), (), s32[]{:S(2)}) async-start(), calls=%async_computation.5 | async-start | bytes 589824 | tf_op jit(solution)/shard_map/reduce_scatter | solution.py:130
  253.1 18.3 %collective-permute-start.2 = (bf16[8,2,24,256]{3,0,2,1:T(8,128)(2,1)S(1)}, bf16[8,2,24,256]{3,0,2,1:T(8,128)(2,1)S(1)}, u32[]{:S(2)}, u32[]{:S(2)}) collective-permute-start(bf16[8,2,24,256]{3,0,2,1:T(8,128)(2,1)S(1)} %get-tuple-element.15), channel_id=1, source_target_pairs={{0,1},{1,2},{2,3},{3,4},{4,5},{5,6},{6,7},{8,9},{9,10},{10,11},{11... | collective-permute-start | bytes 589832 | tf_op jit(solution)/shard_map/ppermute | solution.py:20
  254.4 17.0 %collective-permute-start.3 = (bf16[8,2,24,256]{3,0,2,1:T(8,128)(2,1)S(1)}, bf16[8,2,24,256]{3,0,2,1:T(8,128)(2,1)S(1)}, u32[]{:S(2)}, u32[]{:S(2)}) collective-permute-start(bf16[8,2,24,256]{3,0,2,1:T(8,128)(2,1)S(1)} %get-tuple-element.16), channel_id=1, source_target_pairs={{1,0},{2,1},{3,2},{4,3},{5,4},{6,5},{7,6},{9,8},{10,9},{11,10},{12... | collective-permute-start | bytes 589832 | tf_op jit(solution)/shard_map/ppermute | solution.py:22
  269.6 38.7 %copy-start.1 = (bf16[2,256,768]{2,1,0:T(8,128)(2,1)S(1)}, bf16[2,256,768]{2,1,0:T(8,128)(2,1)}, u32[]{:S(2)}) copy-start(bf16[2,256,768]{2,1,0:T(8,128)(2,1)} %param.11) | copy-start | bytes 2359300
  271.4 36.2 %copy-start.15 = (bf16[2,32,768]{2,0,1:T(2,128)(2,1)S(1)}, bf16[2,32,768]{2,0,1:T(2,128)(2,1)}, u32[]{:S(2)}) copy-start(bf16[2,32,768]{2,0,1:T(2,128)(2,1)} %all-reduce.6.cloned.1.call-done) | copy-start | bytes 294916
  (4 other events, 5.7 us)
Sparse Core Ops, SparseCore 0:
  228.0 41.5 all-reduce.5
Sparse Core Ops, SparseCore 1:
  230.7 30.6 reduce-scatter.1
where the time goes:
time: 319 us; the launch traced here: 316 us
  matrix products  105 us (33%)
  blocking collectives  103 us (32%)
  local copies, waits for them, and re-layouts  48 us (15%)
  between operations  18.8 us (6%)
  starting transfers between devices  14.6 us (5%)
  waiting for transfers between devices  14 us (4%)
  other arithmetic  12.7 us (4%)
    unnamed x1, blocking collectives  63 us
    dot_general x2, matrix products, body(): jnp.einsum('bt,bgc,bge->tce', type_wide, all_feats.astype(f32), d_qkv, pr...  52.1 us
    psum x1, blocking collectives, body(): lax.psum(part_out.astype(jnp.bfloat16), 'agent').astype(jnp.float32)  15.3 us
    psum x1, blocking collectives, body(): square_sum = lax.psum(local_squares, 'tile')  14.1 us
    psum x1, waiting for transfers between devices, body(): lax.psum(part_qkv.astype(jnp.bfloat16), 'agent').astype(jnp.float32)  13.9 us
    dot_general x1, matrix products, body(): jnp.einsum('bge,bce->bgc', d_qkv, wqkv_all.astype(f32), precision=highest)  12.5 us
    all_to_all x1, blocking collectives, body(): lax.all_to_all(d_part, 'agent', split_axis=0, concat_axis=1, tiled=True)  10.1 us
    unnamed x45, local copies, waits for them, and re-layouts  8.71 us
  transfers between devices with their start and end apart: 8, of which 1 were waited for; matrix products, arithmetic and copies ran while one was open for 13% of the time, Pallas kernels for 0%

commit v1 on v0

v1 whole, which is shorter than its diff:
```python
import functools
import math

import jax
import jax.numpy as jnp
from jax import lax
from jax.experimental import pallas as pl
from jax.experimental.pallas import tpu as pltpu
from jax.sharding import PartitionSpec as P

HEADS = 8
MAXOFF = 2
F32 = jnp.float32
BF16 = jnp.bfloat16


def dot(a, b, ca, cb):
    return lax.dot_general(a, b, (((ca,), (cb,)), ((), ())), preferred_element_type=F32)


def layer_kernel(agents, cells, x_ref, g_ref, types_ref, valid_ref, wqkv_ref, wout_ref, dx_ref, raw_ref,
                 qkv_s, da_s, att_s, dqkv_s, head_s):
    channels = x_ref.shape[1]
    head = channels // HEADS
    scale = head ** (-0.5)
    wide = HEADS * agents
    group = max(1, 256 // agents)
    while cells % group:
        group -= 1
    rows = group * agents
    is_one = types_ref[...] == 1
    type_wide = jnp.broadcast_to(is_one, (agents, channels)).astype(F32)
    type_rows = jnp.concatenate([type_wide] * group, axis=0)
    owner = lax.broadcasted_iota(jnp.int32, (wide, channels), 0) // agents
    lane = lax.broadcasted_iota(jnp.int32, (wide, channels), 1) // head
    head_s[...] = (owner == lane).astype(F32).astype(BF16)

    def project(i, _):
        at = pl.ds(pl.multiple_of(i * rows, rows), rows)
        x = x_ref[at, :]
        g = g_ref[at, :]
        for j in range(3):
            cols = slice(j * channels, (j + 1) * channels)
            a = dot(x, wqkv_ref[0, :, cols], 1, 0)
            b = dot(x, wqkv_ref[1, :, cols], 1, 0)
            qkv_s[at, cols] = jnp.where(type_rows > 0.5, b, a).astype(BF16)
        a = dot(g, wout_ref[0], 1, 1)
        b = dot(g, wout_ref[1], 1, 1)
        da_s[at, :] = jnp.where(type_rows > 0.5, b, a).astype(BF16)
        return 0

    lax.fori_loop(0, cells // group, project, 0)

    key_id = lax.broadcasted_iota(jnp.int32, (agents, wide), 0)
    query_id = lax.broadcasted_iota(jnp.int32, (agents, wide), 1) % agents
    allowed = (jnp.broadcast_to(valid_ref[...], (agents, wide)) == 1) | (key_id == query_id)
    lane_head = lax.broadcasted_iota(jnp.int32, (agents, channels), 1) // head

    def own_heads(full):
        out = full[:agents]
        for h in range(1, HEADS):
            out = jnp.where(lane_head == h, full[h * agents:(h + 1) * agents], out)
        return out

    def attend(i, _):
        at = pl.ds(pl.multiple_of(i * agents, agents), agents)
        q = qkv_s[at, :channels]
        k = qkv_s[at, channels:2 * channels]
        v = qkv_s[at, 2 * channels:]
        da = da_s[at, :]
        mask = head_s[...]
        qx = jnp.concatenate([q] * HEADS, axis=0) * mask
        dax = jnp.concatenate([da] * HEADS, axis=0) * mask
        scores = dot(k, qx, 1, 1) * scale
        raised = jnp.where(allowed, jnp.exp(scores), 0.0)
        prob = raised / jnp.sum(raised, axis=0, keepdims=True)
        low = prob.astype(BF16)
        pg = dot(v, dax, 1, 1)
        sg = (prob * (pg - jnp.sum(prob * pg, axis=0, keepdims=True)) * scale).astype(BF16)
        dqkv_s[at, channels:2 * channels] = dot(sg, qx, 1, 0).astype(BF16)
        dqkv_s[at, 2 * channels:] = dot(low, dax, 1, 0).astype(BF16)
        att_s[at, :] = own_heads(dot(low, v, 0, 0)).astype(BF16)
        dqkv_s[at, :channels] = own_heads(dot(sg, k, 0, 0)).astype(BF16)
        return 0

    lax.fori_loop(0, cells, attend, 0, unroll=4)

    def back(i, _):
        at = pl.ds(pl.multiple_of(i * rows, rows), rows)
        d = dqkv_s[at, :]
        a = dot(d, wqkv_ref[0], 1, 1)
        b = dot(d, wqkv_ref[1], 1, 1)
        dx_ref[at, :] = jnp.where(type_rows > 0.5, b, a).astype(BF16)
        return 0

    lax.fori_loop(0, cells // group, back, 0)

    ones = jnp.concatenate([type_wide.astype(BF16)] * cells, axis=0)
    for t in range(2):
        pick = ones if t else (1 - ones).astype(BF16)
        xt = x_ref[...] * pick
        for j in range(3):
            cols = slice(j * channels, (j + 1) * channels)
            raw_ref[t, :, cols] = dot(xt, dqkv_s[:, cols], 0, 0).astype(BF16)
        raw_ref[t, :, 3 * channels:] = dot(att_s[...] * pick, g_ref[...], 0, 0).astype(BF16)


def layer(x, g, types, valid, w_qkv, w_out):
    cells, agents, channels = x.shape
    n = cells * agents
    vmem = pl.BlockSpec(memory_space=pltpu.VMEM)
    dx, raw = pl.pallas_call(
        functools.partial(layer_kernel, agents, cells),
        out_shape=(
            jax.ShapeDtypeStruct((n, channels), BF16),
            jax.ShapeDtypeStruct((2, channels, 4 * channels), BF16),
        ),
        in_specs=[vmem] * 6,
        out_specs=(vmem, vmem),
        scratch_shapes=[
            pltpu.VMEM((n, 3 * channels), BF16),
            pltpu.VMEM((n, channels), BF16),
            pltpu.VMEM((n, channels), BF16),
            pltpu.VMEM((n, 3 * channels), BF16),
            pltpu.VMEM((HEADS * agents, channels), BF16),
        ],
        compiler_params=pltpu.CompilerParams(vmem_limit_bytes=40 * 2**20),
        cost_estimate=pl.CostEstimate(flops=8 * 10**9, bytes_accessed=5 * 10**6, transcendentals=n * 256),
    )(x.reshape(n, channels), g.reshape(n, channels), types[:, None], valid[:, None], w_qkv, w_out)
    return dx.reshape(cells, agents, channels), raw


def with_halo(cells, width):
    count = lax.axis_size("tile")
    ends = count - 1
    head = cells[:, :width]
    tail = cells[:, cells.shape[1] - width:]
    return jnp.concatenate(
        [
            lax.ppermute(tail, "tile", [(i, i + 1) for i in range(ends)]),
            cells,
            lax.ppermute(head, "tile", [(i + 1, i) for i in range(ends)]),
        ],
        axis=1,
    )


def relocate(rimmed, offsets, direction):
    padded = jnp.pad(rimmed, ((0, 0), (0, 0), (MAXOFF, MAXOFF), (0, 0)))
    row_count = rimmed.shape[1] - 2 * MAXOFF
    col_count = rimmed.shape[2]
    planes = []
    for a in range(rimmed.shape[0]):
        start = (MAXOFF + direction * offsets[a, 0], MAXOFF + direction * offsets[a, 1], jnp.int32(0))
        planes.append(lax.dynamic_slice(padded[a], start, (row_count, col_count, rimmed.shape[3])))
    return planes


def body(feats, types, valid, offsets, w_qkv, w_out, d_out):
    own, row_count, col_count, channels = feats.shape
    parts = lax.axis_size("agent")
    tiles = lax.axis_size("tile")
    local = row_count * col_count
    first = lax.axis_index("agent") * own
    own_offsets = lax.dynamic_slice_in_dim(offsets, first, own, 0)
    grads = jnp.swapaxes(d_out.reshape(own, local, channels), 0, 1)
    all_grads = lax.all_to_all(grads, "agent", split_axis=0, concat_axis=1, tiled=True)
    planes = relocate(with_halo(feats, MAXOFF), own_offsets, 1)
    warped = jnp.stack([p.reshape(local, channels) for p in planes], axis=1)
    all_feats = lax.all_to_all(warped, "agent", split_axis=0, concat_axis=1, tiled=True)
    d_part, raw = layer(all_feats, all_grads, types, valid, w_qkv, w_out)
    returned = lax.all_to_all(d_part, "agent", split_axis=1, concat_axis=0, tiled=True)
    d_warped = jnp.swapaxes(returned, 0, 1).reshape(own, row_count, col_count, channels)
    d_feats = jnp.stack(relocate(with_halo(d_warped, MAXOFF), own_offsets, -1))

    width = raw.shape[2]
    rows = channels // tiles
    chips = tiles // 2
    pairs = [[2 * i, 2 * i + 1] for i in range(chips)]
    lines = [[2 * i + c for i in range(chips)] for c in range(2)]
    part = raw.reshape(2, chips, 2, rows, width).transpose(2, 0, 1, 3, 4)
    part = lax.all_to_all(part, "tile", 0, 0, axis_index_groups=pairs, tiled=True)
    part = jnp.sum(part.astype(F32), axis=0).astype(BF16)
    part = part.reshape(2, chips, rows, parts, width // parts).transpose(3, 1, 0, 2, 4)
    part = lax.all_to_all(part, "agent", 0, 0, tiled=True)
    part = jnp.sum(part.astype(F32), axis=0).astype(BF16)
    part = lax.all_to_all(part, "tile", 0, 0, axis_index_groups=lines, tiled=True)
    part = jnp.sum(part.astype(F32), axis=0)
    squares = jnp.full((8, 128), jnp.sum(part * part), F32)
    total = jnp.sum(lax.all_gather(squares, ("agent", "tile"))[:, 0, 0])
    whole = lax.all_gather(part, "agent")
    limit = math.sqrt(8.0 * channels * channels)
    factor = limit / jnp.maximum(jnp.sqrt(total), limit)
    whole = whole.transpose(1, 2, 0, 3).reshape(2, rows, width) * factor
    return (d_feats, whole[..., :3 * channels], whole[..., 3 * channels:])


def solution(mesh):
    placed = (
        P("agent", "tile", None, None),
        P(),
        P(),
        P(),
        P(),
        P(),
        P("agent", "tile", None, None),
    )
    return jax.shard_map(
        body,
        mesh=mesh,
        in_specs=placed,
        out_specs=(P("agent", "tile", None, None), P(None, "tile", None), P(None, "tile", None)),
        check_vma=False,
    )
```

time: 319 us -> 160 us (0.50)
  matrix products: 105 us -> 0 us
  blocking collectives: 103 us -> 48.4 us
  local copies, waits for them, and re-layouts: 48 us -> 10.8 us
  starting transfers between devices: 14.6 us -> 34.6 us
  between operations: 18.8 us -> 32 us
  Pallas kernels: 0 us -> 11.5 us
  other arithmetic: 12.7 us -> 2.71 us
  waiting for transfers between devices: 14 us -> 18.9 us
    dot_general x12 -> x0, matrix products: 105 us -> none  [the longest x2 52.1 us: body(): jnp.einsum('bt,bgc,bge->tce', type_wide, all_feats.astype(f32), d_qkv, pr...]
    psum x2 -> x0, blocking collectives: 29.4 us -> none  [the longest x1 15.3 us: body(): lax.psum(part_out.astype(jnp.bfloat16), 'agent').astype(jnp.float32)]
    unnamed x1, blocking collectives: 63 us -> 38.9 us
    all_to_all x2 -> x6, starting transfers between devices: 9.19 us -> 28.2 us  [the longest x1 8.83 us: body(): lax.all_to_all(part, 'tile', 0, 0, axis_index_groups=lines, tiled=True)]
    all_to_all x2 -> x6, waiting for transfers between devices: 0.01 us -> 18.9 us  [the longest x1 7.18 us: body(): lax.all_to_all(warped, 'agent', split_axis=0, concat_axis=1, tiled=True)]
    psum x1 -> x0, waiting for transfers between devices: 13.9 us -> none  [body(): lax.psum(part_qkv.astype(jnp.bfloat16), 'agent').astype(jnp.float32)]
    gather x4 -> x0, local copies, waits for them, and re-layouts: 13.5 us -> none  [the longest x1 6.57 us: body(): wqkv_all = jnp.take(w_qkv, types, axis=0)]
    pallas_call x0 -> x1, Pallas kernels: none -> 11.5 us  [layer(): pl.pallas_call(functools.partial(layer_kernel, agents, cells), out_shape=...]
  transfers between devices with their start and end apart: 8 -> 10, of which waited for: 1 -> 4; matrix products, arithmetic and copies ran while one was open for 13% -> 5% of each run, Pallas kernels for 0% -> 0%
where the time goes in v1:
time: 160 us; the launch traced here: 159 us
  blocking collectives  48.4 us (30%)
  starting transfers between devices  34.6 us (22%)
  between operations  32 us (20%)
  waiting for transfers between devices  18.9 us (12%)
  Pallas kernels  11.5 us (7%)
  local copies, waits for them, and re-layouts  10.8 us (7%)
  other arithmetic  2.71 us (2%)
    unnamed x1, blocking collectives  38.9 us
    pallas_call x1, Pallas kernels, layer(): pl.pallas_call(functools.partial(layer_kernel, agents, cells), out_shape=...  11.5 us
    all_gather x1, blocking collectives, body(): whole = lax.all_gather(part, 'agent')  9.45 us
    all_to_all x1, starting transfers between devices, body(): lax.all_to_all(part, 'tile', 0, 0, axis_index_groups=lines, tiled=True)  8.83 us
    all_to_all x1, waiting for transfers between devices, body(): lax.all_to_all(warped, 'agent', split_axis=0, concat_axis=1, tiled=True)  7.18 us
    all_to_all x1, waiting for transfers between devices, body(): lax.all_to_all(d_part, 'agent', split_axis=1, concat_axis=0, tiled=True)  5.63 us
    all_to_all x1, waiting for transfers between devices, body(): lax.all_to_all(part, 'tile', 0, 0, axis_index_groups=lines, tiled=True)  4.96 us
    all_to_all x1, starting transfers between devices, body(): lax.all_to_all(grads, 'agent', split_axis=0, concat_axis=1, tiled=True)  4.55 us
  transfers between devices with their start and end apart: 10, of which 4 were waited for; matrix products, arithmetic and copies ran while one was open for 5% of the time, Pallas kernels for 0%

profile of v1, /device:TPU:0, one launch (start us, length us, event | category | flops | bytes accessed | tf_op | source)
XLA Modules:
  0.0 158.9 jit_solution(14618716777447605694)
XLA Ops:
  0.7 1.1 fusion.9
  1.8 2.5 %collective-permute-start = (bf16[8,2,24,256]{3,2,1,0:T(8,128)(2,1)S(1)}, bf16[8,2,24,256]{3,2,1,0:T(8,128)(2,1)S(1)}, u32[]{:S(2)}, u32[]{:S(2)}) collective-permute-start(bf16[8,2,24,256]{3,2,1,0:T(8,128)(2,1)S(1)} %get-tuple-element.25), channel_id=1, source_target_pairs={{0,1},{1,2},{2,3},{3,4},{4,5},{5,6},{6,7},{8,9},{9,10},{10,11},{11... | collective-permute-start | bytes 589832 | tf_op jit(solution)/shard_map/ppermute | solution.py:140
  4.3 1.3 collective-permute-start.1
  5.6 1.0 copy.81
  6.6 4.5 %all-to-all-start.1 = ((bf16[96,8,256]{2,1,0:T(8,128)(2,1)}), bf16[96,8,256]{2,1,0:T(8,128)(2,1)S(1)}, u32[]{:S(2)}, u32[]{:S(2)}) async-start(bf16[96,8,256]{2,1,0:T(8,128)(2,1)} %bitcast.44), calls=%async_computation.1 | async-start | bytes 786432 | tf_op jit(solution)/shard_map/all_to_all | solution.py:167
  33.0 1.0 copy.79
  33.9 4.3 %all-to-all-start = ((bf16[96,8,256]{2,1,0:T(8,128)(2,1)}), bf16[96,8,256]{2,1,0:T(8,128)(2,1)S(1)}, u32[]{:S(2)}, u32[]{:S(2)}) async-start(bf16[96,8,256]{2,1,0:T(8,128)(2,1)} %copy.79), calls=%async_computation | async-start | bytes 786432 | tf_op jit(solution)/shard_map/all_to_all | solution.py:170
  38.5 7.2 %all-to-all-done = bf16[96,8,256]{2,1,0:T(8,128)(2,1)S(1)} async-done(((bf16[96,8,256]{2,1,0:T(8,128)(2,1)}), bf16[96,8,256]{2,1,0:T(8,128)(2,1)S(1)}, u32[]{:S(2)}, u32[]{:S(2)}) %all-to-all-start) | async-done | bytes 393248 | tf_op jit(solution)/shard_map/all_to_all | solution.py:170
  45.7 11.5 %shard_map.94 = (bf16[768,256]{1,0:T(8,128)(2,1)S(1)}, bf16[2,256,1024]{2,1,0:T(8,128)(2,1)S(1)}) custom-call(bf16[768,256]{1,0:T(8,128)(2,1)S(1)} %bitcast.110, bf16[768,256]{1,0:T(8,128)(2,1)S(1)} %bitcast.108, s32[32,1]{1,0:T(8,128)S(1)} %copy.83.types_ref, s32[32,1]{1,0:T(8,128)S(1)} %copy.84.valid_ref, bf16[2,256,768]{2,1,0:T(8,128)(2,1)S(1)} %copy-done.1, ...), custom_call_target="tpu_custom_call" | custom-call | flops 8000000000 | bytes 5000000 | tf_op jit(solution)/shard_map/pallas_call | solution.py:112
  57.3 1.1 copy.103
  58.4 3.6 %all-to-all-start.3 = ((bf16[2,2,4,32,1024]{4,3,2,1,0:T(8,128)(2,1)}), bf16[2,2,4,32,1024]{4,3,2,1,0:T(8,128)(2,1)S(1)}, u32[]{:S(2)}, u32[]{:S(2)}) async-start(bf16[2,2,4,32,1024]{4,3,2,1,0:T(8,128)(2,1)} %bitcast.106), calls=%async_computation.3 | async-start | bytes 2097152 | tf_op jit(solution)/shard_map/all_to_all | solution.py:182
  61.9 1.0 copy.85
  62.9 1.1 all-to-all-done.3
  64.0 3.5 %all-to-all-start.2 = ((bf16[24,32,256]{2,0,1:T(8,128)(2,1)}), bf16[24,32,256]{2,0,1:T(8,128)(2,1)S(1)}, u32[]{:S(2)}, u32[]{:S(2)}) async-start(bf16[24,32,256]{2,0,1:T(8,128)(2,1)} %copy.85), calls=%async_computation.2 | async-start | bytes 786432 | tf_op jit(solution)/shard_map/all_to_all | solution.py:172
  68.2 0.9 copy.92
  69.0 5.6 %all-to-all-done.2 = bf16[24,32,256]{2,0,1:T(8,128)(2,1)S(1)} async-done(((bf16[24,32,256]{2,0,1:T(8,128)(2,1)}), bf16[24,32,256]{2,0,1:T(8,128)(2,1)S(1)}, u32[]{:S(2)}, u32[]{:S(2)}) %all-to-all-start.2) | async-done | bytes 393248 | tf_op jit(solution)/shard_map/all_to_all | solution.py:172
  74.7 3.5 %all-to-all-start.4 = ((bf16[4,4,2,32,256]{4,3,1,2,0:T(8,128)(2,1)}), bf16[4,4,2,32,256]{4,3,1,2,0:T(8,128)(2,1)S(1)}, u32[]{:S(2)}, u32[]{:S(2)}) async-start(bf16[4,4,2,32,256]{4,3,1,2,0:T(8,128)(2,1)} %copy.92), calls=%async_computation.4 | async-start | bytes 1048576 | tf_op jit(solution)/shard_map/all_to_all | solution.py:185
  78.2 1.3 collective-permute-start.2
  79.5 1.3 collective-permute-start.3
  91.7 8.8 %all-to-all-start.5 = ((bf16[4,2,32,256]{3,2,1,0:T(8,128)(2,1)}), bf16[4,2,32,256]{3,2,1,0:T(8,128)(2,1)S(1)}, u32[]{:S(2)}, u32[]{:S(2)}) async-start(bf16[4,2,32,256]{3,2,1,0:T(8,128)(2,1)} %copy.93), calls=%async_computation.5 | async-start | bytes 262144 | tf_op jit(solution)/shard_map/all_to_all | solution.py:187
  101.5 5.0 %all-to-all-done.5 = bf16[4,2,32,256]{3,2,1,0:T(8,128)(2,1)S(1)} async-done(((bf16[4,2,32,256]{3,2,1,0:T(8,128)(2,1)}), bf16[4,2,32,256]{3,2,1,0:T(8,128)(2,1)S(1)}, u32[]{:S(2)}, u32[]{:S(2)}) %all-to-all-start.5) | async-done | bytes 131104 | tf_op jit(solution)/shard_map/all_to_all | solution.py:187
  107.1 0.8 dynamic-update-slice
  107.8 9.5 %all-gather = f32[8,32,256]{2,1,0:T(8,128)S(1)} all-gather(f32[2,32,256]{2,1,0:T(8,128)S(1)} %convert_reduce_fusion), channel_id=3, replica_groups=mesh['agent'=4,'tile'=8] {'agent'}, dimensions={0}, use_global_device_ids=true | all-gather | bytes 327680 | tf_op jit(solution)/shard_map/all_gather | solution.py:191
  117.3 38.9 %all-reduce.2 = f32[32]{0:T(128)S(1)} all-reduce(f32[32]{0:T(128)S(1)} %dynamic-update-slice), channel_id=2, replica_groups=mesh['agent'=4,'tile'=8] {'agent','tile'}, use_global_device_ids=true, to_apply=%add.2 | all-reduce | flops 32 | bytes 256
  (65 shorter events, 6.8 us)
Async XLA Ops:
  0.6 10.5 %copy-start = (s32[32,2]{0,1:T(2,128)S(1)}, s32[32,2]{0,1:T(2,128)}, u32[]{:S(2)}) copy-start(s32[32,2]{0,1:T(2,128)} %param.10) | copy-start | bytes 772
  0.6 4.9 %copy-start.4 = (bf16[8,4,24,256]{3,2,1,0:T(8,128)(2,1)S(1)}, bf16[8,4,24,256]{3,2,1,0:T(8,128)(2,1)}, u32[]{:S(2)}) copy-start(bf16[8,4,24,256]{3,2,1,0:T(8,128)(2,1)} %param.13) | copy-start | bytes 1179652
  1.8 30.2 %copy-start.3 = (bf16[8,4,24,256]{3,2,1,0:T(8,128)(2,1)S(1)}, bf16[8,4,24,256]{3,2,1,0:T(8,128)(2,1)}, u32[]{:S(2)}) copy-start(bf16[8,4,24,256]{3,2,1,0:T(8,128)(2,1)} %param.7) | copy-start | bytes 1179652
  1.8 30.2 %collective-permute-start = (bf16[8,2,24,256]{3,2,1,0:T(8,128)(2,1)S(1)}, bf16[8,2,24,256]{3,2,1,0:T(8,128)(2,1)S(1)}, u32[]{:S(2)}, u32[]{:S(2)}) collective-permute-start(bf16[8,2,24,256]{3,2,1,0:T(8,128)(2,1)S(1)} %get-tuple-element.25), channel_id=1, source_target_pairs={{0,1},{1,2},{2,3},{3,4},{4,5},{5,6},{6,7},{8,9},{9,10},{10,11},{11... | collective-permute-start | bytes 589832 | tf_op jit(solution)/shard_map/ppermute | solution.py:140
  4.3 27.7 %collective-permute-start.1 = (bf16[8,2,24,256]{3,2,1,0:T(8,128)(2,1)S(1)}, bf16[8,2,24,256]{3,2,1,0:T(8,128)(2,1)S(1)}, u32[]{:S(2)}, u32[]{:S(2)}) collective-permute-start(bf16[8,2,24,256]{3,2,1,0:T(8,128)(2,1)S(1)} %get-tuple-element.26), channel_id=1, source_target_pairs={{1,0},{2,1},{3,2},{4,3},{5,4},{6,5},{7,6},{9,8},{10,9},{11,10},{12... | collective-permute-start | bytes 589832 | tf_op jit(solution)/shard_map/ppermute | solution.py:142
  6.6 27.4 %all-to-all-start.1 = ((bf16[96,8,256]{2,1,0:T(8,128)(2,1)}), bf16[96,8,256]{2,1,0:T(8,128)(2,1)S(1)}, u32[]{:S(2)}, u32[]{:S(2)}) async-start(bf16[96,8,256]{2,1,0:T(8,128)(2,1)} %bitcast.44), calls=%async_computation.1 | async-start | bytes 786432 | tf_op jit(solution)/shard_map/all_to_all | solution.py:167
  32.8 5.4 %copy-start.6 = (s32[32]{0:T(128)S(1)}, s32[32]{0:T(128)}, u32[]{:S(2)}) copy-start(s32[32]{0:T(128)} %param.8) | copy-start | bytes 388
  32.9 5.5 %copy-start.7 = (s32[32]{0:T(128)S(1)}, s32[32]{0:T(128)}, u32[]{:S(2)}) copy-start(s32[32]{0:T(128)} %param.9) | copy-start | bytes 388
  33.9 11.8 %copy-start.1 = (bf16[2,256,768]{2,1,0:T(8,128)(2,1)S(1)}, bf16[2,256,768]{2,1,0:T(8,128)(2,1)}, u32[]{:S(2)}) copy-start(bf16[2,256,768]{2,1,0:T(8,128)(2,1)} %wqkv_ref.1) | copy-start | bytes 2359300
  33.9 11.8 %copy-start.2 = (bf16[2,256,256]{2,1,0:T(8,128)(2,1)S(1)}, bf16[2,256,256]{2,1,0:T(8,128)(2,1)}, u32[]{:S(2)}) copy-start(bf16[2,256,256]{2,1,0:T(8,128)(2,1)} %wout_ref.1) | copy-start | bytes 786436
  33.9 11.7 %all-to-all-start = ((bf16[96,8,256]{2,1,0:T(8,128)(2,1)}), bf16[96,8,256]{2,1,0:T(8,128)(2,1)S(1)}, u32[]{:S(2)}, u32[]{:S(2)}) async-start(bf16[96,8,256]{2,1,0:T(8,128)(2,1)} %copy.79), calls=%async_computation | async-start | bytes 786432 | tf_op jit(solution)/shard_map/all_to_all | solution.py:170
  58.4 5.7 %all-to-all-start.3 = ((bf16[2,2,4,32,1024]{4,3,2,1,0:T(8,128)(2,1)}), bf16[2,2,4,32,1024]{4,3,2,1,0:T(8,128)(2,1)S(1)}, u32[]{:S(2)}, u32[]{:S(2)}) async-start(bf16[2,2,4,32,1024]{4,3,2,1,0:T(8,128)(2,1)} %bitcast.106), calls=%async_computation.3 | async-start | bytes 2097152 | tf_op jit(solution)/shard_map/all_to_all | solution.py:182
  64.0 10.6 %all-to-all-start.2 = ((bf16[24,32,256]{2,0,1:T(8,128)(2,1)}), bf16[24,32,256]{2,0,1:T(8,128)(2,1)S(1)}, u32[]{:S(2)}, u32[]{:S(2)}) async-start(bf16[24,32,256]{2,0,1:T(8,128)(2,1)} %copy.85), calls=%async_computation.2 | async-start | bytes 786432 | tf_op jit(solution)/shard_map/all_to_all | solution.py:172
  74.7 16.3 %all-to-all-start.4 = ((bf16[4,4,2,32,256]{4,3,1,2,0:T(8,128)(2,1)}), bf16[4,4,2,32,256]{4,3,1,2,0:T(8,128)(2,1)S(1)}, u32[]{:S(2)}, u32[]{:S(2)}) async-start(bf16[4,4,2,32,256]{4,3,1,2,0:T(8,128)(2,1)} %copy.92), calls=%async_computation.4 | async-start | bytes 1048576 | tf_op jit(solution)/shard_map/all_to_all | solution.py:185
  78.2 22.4 %collective-permute-start.2 = (bf16[8,2,24,256]{3,2,1,0:T(8,128)(2,1)S(1)}, bf16[8,2,24,256]{3,2,1,0:T(8,128)(2,1)S(1)}, u32[]{:S(2)}, u32[]{:S(2)}) collective-permute-start(bf16[8,2,24,256]{3,2,1,0:T(8,128)(2,1)S(1)} %get-tuple-element.23), channel_id=1, source_target_pairs={{0,1},{1,2},{2,3},{3,4},{4,5},{5,6},{6,7},{8,9},{9,10},{10,11},{11... | collective-permute-start | bytes 589832 | tf_op jit(solution)/shard_map/ppermute | solution.py:140
  79.5 21.0 %collective-permute-start.3 = (bf16[8,2,24,256]{3,2,1,0:T(8,128)(2,1)S(1)}, bf16[8,2,24,256]{3,2,1,0:T(8,128)(2,1)S(1)}, u32[]{:S(2)}, u32[]{:S(2)}) collective-permute-start(bf16[8,2,24,256]{3,2,1,0:T(8,128)(2,1)S(1)} %get-tuple-element.24), channel_id=1, source_target_pairs={{1,0},{2,1},{3,2},{4,3},{5,4},{6,5},{7,6},{9,8},{10,9},{11,10},{12... | collective-permute-start | bytes 589832 | tf_op jit(solution)/shard_map/ppermute | solution.py:142
  91.7 14.7 %all-to-all-start.5 = ((bf16[4,2,32,256]{3,2,1,0:T(8,128)(2,1)}), bf16[4,2,32,256]{3,2,1,0:T(8,128)(2,1)S(1)}, u32[]{:S(2)}, u32[]{:S(2)}) async-start(bf16[4,2,32,256]{3,2,1,0:T(8,128)(2,1)} %copy.93), calls=%async_computation.5 | async-start | bytes 262144 | tf_op jit(solution)/shard_map/all_to_all | solution.py:187
  101.5 57.5 %copy-start.5 = (bf16[8,4,24,256]{3,2,1,0:T(8,128)(2,1)}, bf16[8,4,24,256]{3,2,1,0:T(8,128)(2,1)S(1)}, u32[]{:S(2)}) copy-start(bf16[8,4,24,256]{3,2,1,0:T(8,128)(2,1)S(1)} %dynamic-slice_dynamic-update-slice_fusion) | copy-start | bytes 1179652

commit v2 on v1

v2 whole, which is shorter than its diff:
```python
import functools
import math

import jax
import jax.numpy as jnp
from jax import lax
from jax.experimental import pallas as pl
from jax.experimental.pallas import tpu as pltpu
from jax.sharding import PartitionSpec as P

HEADS = 8
MAXOFF = 2
F32 = jnp.float32
BF16 = jnp.bfloat16


def dot(a, b, ca, cb):
    return lax.dot_general(a, b, (((ca,), (cb,)), ((), ())), preferred_element_type=F32)


def layer_kernel(agents, cells, own, tiles, x_ref, g_ref, types_ref, valid_ref, wqkv_ref, wout_ref, dx_ref, raw_ref,
                 qkv_s, da_s, att_s, dqkv_s, head_s):
    channels = x_ref.shape[1]
    head = channels // HEADS
    scale = head ** (-0.5)
    wide = HEADS * agents
    group = max(1, 256 // agents)
    while cells % group:
        group -= 1
    rows = group * agents
    is_one = types_ref[...] == 1
    type_wide = jnp.broadcast_to(is_one, (agents, channels)).astype(F32)
    type_rows = jnp.concatenate([type_wide] * group, axis=0)
    owner = lax.broadcasted_iota(jnp.int32, (wide, channels), 0) // agents
    lane = lax.broadcasted_iota(jnp.int32, (wide, channels), 1) // head
    head_s[...] = (owner == lane).astype(F32).astype(BF16)

    def project(i, _):
        at = pl.ds(pl.multiple_of(i * rows, rows), rows)
        x = x_ref[at, :]
        g = g_ref[at, :]
        for j in range(3):
            cols = slice(j * channels, (j + 1) * channels)
            a = dot(x, wqkv_ref[0, :, cols], 1, 0)
            b = dot(x, wqkv_ref[1, :, cols], 1, 0)
            qkv_s[at, cols] = jnp.where(type_rows > 0.5, b, a).astype(BF16)
        a = dot(g, wout_ref[0], 1, 1)
        b = dot(g, wout_ref[1], 1, 1)
        da_s[at, :] = jnp.where(type_rows > 0.5, b, a).astype(BF16)
        return 0

    lax.fori_loop(0, cells // group, project, 0)

    key_id = lax.broadcasted_iota(jnp.int32, (agents, wide), 0)
    query_id = lax.broadcasted_iota(jnp.int32, (agents, wide), 1) % agents
    allowed = (jnp.broadcast_to(valid_ref[...], (agents, wide)) == 1) | (key_id == query_id)
    lane_head = lax.broadcasted_iota(jnp.int32, (agents, channels), 1) // head

    def own_heads(full):
        out = full[:agents]
        for h in range(1, HEADS):
            out = jnp.where(lane_head == h, full[h * agents:(h + 1) * agents], out)
        return out

    def attend(i, _):
        at = pl.ds(pl.multiple_of(i * agents, agents), agents)
        q = qkv_s[at, :channels]
        k = qkv_s[at, channels:2 * channels]
        v = qkv_s[at, 2 * channels:]
        da = da_s[at, :]
        mask = head_s[...]
        qx = jnp.concatenate([q] * HEADS, axis=0) * mask
        dax = jnp.concatenate([da] * HEADS, axis=0) * mask
        scores = dot(k, qx, 1, 1) * scale
        raised = jnp.where(allowed, jnp.exp(scores), 0.0)
        prob = raised / jnp.sum(raised, axis=0, keepdims=True)
        low = prob.astype(BF16)
        pg = dot(v, dax, 1, 1)
        sg = (prob * (pg - jnp.sum(prob * pg, axis=0, keepdims=True)) * scale).astype(BF16)
        dqkv_s[at, channels:2 * channels] = dot(sg, qx, 1, 0).astype(BF16)
        dqkv_s[at, 2 * channels:] = dot(low, dax, 1, 0).astype(BF16)
        att_s[at, :] = own_heads(dot(low, v, 0, 0)).astype(BF16)
        dqkv_s[at, :channels] = own_heads(dot(sg, k, 0, 0)).astype(BF16)
        return 0

    lax.fori_loop(0, cells, attend, 0, unroll=4)

    def back(i, _):
        at = pl.ds(pl.multiple_of(i * rows, rows), rows)
        d = dqkv_s[at, :]
        a = dot(d, wqkv_ref[0], 1, 1)
        b = dot(d, wqkv_ref[1], 1, 1)
        full = jnp.where(type_rows > 0.5, b, a).reshape(group, agents, channels)
        for n in range(agents // own):
            part = full[:, n * own:(n + 1) * own].reshape(group * own, channels)
            dx_ref[n, pl.ds(pl.multiple_of(i * group * own, group * own), group * own), :] = part.astype(BF16)
        return 0

    lax.fori_loop(0, cells // group, back, 0)

    ones = jnp.concatenate([type_wide.astype(BF16)] * cells, axis=0)
    share = channels // tiles
    for t in range(2):
        pick = ones if t else (1 - ones).astype(BF16)
        xt = x_ref[...] * pick
        for j in range(4):
            if j < 3:
                full = dot(xt, dqkv_s[:, j * channels:(j + 1) * channels], 0, 0)
            else:
                full = dot(att_s[...] * pick, g_ref[...], 0, 0)
            for i in range(tiles):
                raw_ref[i % 2, j, i // 2, t * share:(t + 1) * share, :] = full[i * share:(i + 1) * share].astype(BF16)


VMEM = pl.BlockSpec(memory_space=pltpu.VMEM)
MESH = pl.DeviceIdType.MESH


def layer(x, g, types, valid, w_qkv, w_out, own, tiles):
    n, channels = x.shape
    agents = types.shape[0]
    cells = n // agents
    parts = agents // own
    return pl.pallas_call(
        functools.partial(layer_kernel, agents, cells, own, tiles),
        out_shape=(
            jax.ShapeDtypeStruct((parts, cells * own, channels), BF16),
            jax.ShapeDtypeStruct((2, 4, tiles // 2, 2 * channels // tiles, channels), BF16),
        ),
        in_specs=[VMEM] * 6,
        out_specs=(VMEM, VMEM),
        scratch_shapes=[
            pltpu.VMEM((n, 3 * channels), BF16),
            pltpu.VMEM((n, channels), BF16),
            pltpu.VMEM((n, channels), BF16),
            pltpu.VMEM((n, 3 * channels), BF16),
            pltpu.VMEM((HEADS * agents, channels), BF16),
        ],
        compiler_params=pltpu.CompilerParams(vmem_limit_bytes=40 * 2**20),
        cost_estimate=pl.CostEstimate(flops=8 * 10**9, bytes_accessed=5 * 10**6, transcendentals=n * 256),
    )(x, g, types[:, None], valid[:, None], w_qkv, w_out)


def one_hot(target, width):
    lanes = lax.broadcasted_iota(jnp.int32, (target.shape[0], width), 1)
    return jnp.where(lanes == target, 1.0, 0.0).astype(BF16)


def greet(others):
    barrier = pltpu.get_barrier_semaphore()
    for there, device in others:
        @pl.when(there)
        def _(device=device):
            pl.semaphore_signal(barrier, inc=1, device_id=device, device_id_type=MESH)
    count = sum(jnp.where(there, 1, 0) for there, _ in others)
    pl.semaphore_wait(barrier, count)


def sender(src, dst, sems, k, device):
    return pltpu.make_async_remote_copy(
        src_ref=src, dst_ref=dst, send_sem=sems.at[0, k], recv_sem=sems.at[1, k], device_id=device, device_id_type=MESH
    )


def front_kernel(parts, tiles, feats_ref, grads_ref, warp_ref, turn_ref, x_ref, g_ref,
                 rim, x_send, g_send, x_recv, g_recv, halo_sem, x_sem, g_sem):
    me, tile = lax.axis_index("agent"), lax.axis_index("tile")
    own, local, channels = feats_ref.shape
    cells = local // parts
    edge = MAXOFF * cells
    inner = rim.shape[1]
    left, right = tile > 0, tile < tiles - 1
    peers = [lax.rem(me + k, parts) for k in range(parts)]
    greet([(left, (me, tile - 1)), (right, (me, tile + 1))] + [(parts > 0, (peers[k], tile)) for k in range(1, parts)])
    to_right = sender(feats_ref.at[:, local - edge:, :], rim.at[:, :edge, :], halo_sem, 0, (me, tile + 1))
    to_left = sender(feats_ref.at[:, :edge, :], rim.at[:, inner - edge:, :], halo_sem, 1, (me, tile - 1))

    @pl.when(right)
    def _():
        to_right.start()

    @pl.when(left)
    def _():
        to_left.start()

    @pl.when(tile == 0)
    def _():
        rim[:, :edge, :] = jnp.zeros((own, edge, channels), BF16)

    @pl.when(tile == tiles - 1)
    def _():
        rim[:, inner - edge:, :] = jnp.zeros((own, edge, channels), BF16)

    rim[:, edge:inner - edge, :] = feats_ref[...]

    def spread(source, target, send, recv, sems):
        copies = []
        for k in (*range(1, parts), 0):
            pick = one_hot(target + peers[k] * cells, source.shape[0])
            value = dot(pick, source, 1, 0).astype(BF16)
            if k == 0:
                recv[me] = value
            else:
                send[k] = value
                copies.append(sender(send.at[k], recv.at[me], sems, k, (peers[k], tile)))
                copies[-1].start()
        return copies

    def gather(copies, recv, out):
        for copy in copies:
            copy.wait()
        pieces = [recv[n].astype(F32).reshape(cells, own, channels) for n in range(parts)]
        out[...] = jnp.concatenate(pieces, axis=1).reshape(cells * own * parts, channels).astype(BF16)

    g_copies = spread(grads_ref[...].reshape(own * local, channels), turn_ref[...], g_send, g_recv, g_sem)

    @pl.when(left)
    def _():
        to_right.wait_recv()
        to_left.wait_send()

    @pl.when(right)
    def _():
        to_left.wait_recv()
        to_right.wait_send()

    x_copies = spread(rim[...].reshape(own * inner, channels), warp_ref[...], x_send, x_recv, x_sem)
    gather(g_copies, g_recv, g_ref)
    gather(x_copies, x_recv, x_ref)


def front(feats, grads, warp, turn, parts, tiles):
    own, local, channels = feats.shape
    cells = local // parts
    inner = local + 2 * MAXOFF * cells
    out = jax.ShapeDtypeStruct((own * local, channels), BF16)
    block = pltpu.VMEM((parts, cells * own, channels), BF16)
    return pl.pallas_call(
        functools.partial(front_kernel, parts, tiles),
        out_shape=(out, out),
        in_specs=[VMEM] * 4,
        out_specs=(VMEM, VMEM),
        scratch_shapes=[
            pltpu.VMEM((own, inner, channels), BF16),
            block, block, block, block,
            pltpu.SemaphoreType.DMA((2, 2)),
            pltpu.SemaphoreType.DMA((2, parts)),
            pltpu.SemaphoreType.DMA((2, parts)),
        ],
        compiler_params=pltpu.CompilerParams(
            collective_id=0, has_side_effects=True, vmem_limit_bytes=40 * 2**20
        ),
    )(feats, grads, warp, turn)


def back_kernel(parts, tiles, dx_ref, raw_ref, turn_ref, df_ref, gq_ref, go_ref,
                rim, pair, first, agent_in, second, line_in, final, every, square, squares,
                dx_sem, halo_sem, pair_sem, agent_sem, line_sem, every_sem, square_sem):
    me, tile = lax.axis_index("agent"), lax.axis_index("tile")
    core, chip = lax.rem(tile, 2), tile // 2
    chips = tiles // 2
    channels = dx_ref.shape[2]
    share = channels // tiles
    left, right = tile > 0, tile < tiles - 1
    peers = [lax.rem(me + k, parts) for k in range(parts)]
    always = parts > 0
    greet(
        [(always, (peers[k], tile)) for k in range(1, parts)]
        + [(always, (me, lax.rem(tile + k, tiles))) for k in range(1, tiles)]
        + [(left, (peers[k], tile - 1)) for k in range(1, parts)]
        + [(right, (peers[k], tile + 1)) for k in range(1, parts)]
    )
    swap = sender(raw_ref.at[1 - core], pair, pair_sem, 0, (me, tile + 1 - 2 * core))
    swap.start()
    low = me < MAXOFF
    next_tile = jnp.where(low, tile - 1, tile + 1)
    next_row = jnp.where(low, me + parts + MAXOFF, me - (parts - MAXOFF))
    there = (next_tile >= 0) & (next_tile < tiles)
    homes = [sender(dx_ref.at[peers[k]], rim.at[me + MAXOFF], dx_sem, k, (peers[k], tile)) for k in range(1, parts)]
    for copy in homes:
        copy.start()
    sides = [sender(dx_ref.at[peers[k]], rim.at[next_row], halo_sem, k, (peers[k], next_tile)) for k in range(parts)]

    @pl.when(there)
    def _():
        for copy in sides:
            copy.start()

    rows = dx_ref.shape[1]

    @pl.when(tile == 0)
    def _():
        rim[:MAXOFF] = jnp.zeros((MAXOFF, rows, channels), BF16)

    @pl.when(tile == tiles - 1)
    def _():
        rim[parts + MAXOFF:] = jnp.zeros((MAXOFF, rows, channels), BF16)

    rim[me + MAXOFF] = dx_ref[me]
    swap.wait()
    first[...] = (raw_ref[core].astype(F32) + pair[...].astype(F32)).astype(BF16)
    agent_copies = [sender(first.at[peers[k]], agent_in.at[k], agent_sem, k, (peers[k], tile)) for k in range(1, parts)]
    for copy in agent_copies:
        copy.start()
    for copy in agent_copies:
        copy.wait()
    total = first[me].astype(F32)
    for k in range(1, parts):
        total = total + agent_in[k].astype(F32)
    second[...] = total.astype(BF16)
    line_copies = []
    for k in range(1, chips):
        other = lax.rem(chip + k, chips)
        line_copies.append(sender(second.at[other], line_in.at[k], line_sem, k, (me, 2 * other + core)))
        line_copies[-1].start()

    for copy in homes:
        copy.wait()
    for k in range(parts):
        origin = lax.rem(me + parts - k, parts)
        arrives = jnp.where(origin < MAXOFF, tile + 1, tile - 1)

        @pl.when((arrives >= 0) & (arrives < tiles))
        def _(k=k):
            sides[k].wait_recv()

        @pl.when(there)
        def _(k=k):
            sides[k].wait_send()

    source = rim[...].reshape(rim.shape[0] * rows, channels)
    own, local = df_ref.shape[:2]
    for i in range(0, own, 2):
        pick = one_hot(turn_ref[i * local:(i + 2) * local, :], source.shape[0])
        df_ref[i:i + 2] = dot(pick, source, 1, 0).reshape(2, local, channels).astype(BF16)

    for copy in line_copies:
        copy.wait()
    total = second[chip].astype(F32)
    for k in range(1, chips):
        total = total + line_in[k].astype(F32)
    final[...] = total.astype(BF16)
    every[me] = total.astype(BF16)
    every_copies = [sender(final, every.at[me], every_sem, k, (peers[k], tile)) for k in range(1, parts)]
    for copy in every_copies:
        copy.start()
    for copy in every_copies:
        copy.wait()
    whole = every[...].astype(F32)
    summed = jnp.sum(whole * whole, axis=0)
    summed = jnp.sum(jnp.sum(summed, axis=0, keepdims=True), axis=1, keepdims=True)
    spread = jnp.broadcast_to(summed, (8, 128))
    square[...] = spread
    squares[tile] = spread
    square_copies = [
        sender(square, squares.at[tile], square_sem, k, (me, lax.rem(tile + k, tiles))) for k in range(1, tiles)
    ]
    for copy in square_copies:
        copy.start()
    for copy in square_copies:
        copy.wait()
    norm = jnp.sqrt(jnp.sum(squares[...], axis=0)[:1, :1])
    limit = math.sqrt(8.0 * channels * channels)
    factor = limit / jnp.maximum(norm, limit)
    for t in range(2):
        for j in range(4):
            piece = every[j].astype(F32)[t * share:(t + 1) * share] * factor
            if j < 3:
                gq_ref[t, :, j * channels:(j + 1) * channels] = piece
            else:
                go_ref[t] = piece


def back(dx, raw, turn, own, tiles):
    parts, rows, channels = dx.shape
    local = parts * rows // own
    share = channels // tiles
    chips = tiles // 2
    dma = lambda n: pltpu.SemaphoreType.DMA((2, n))
    return pl.pallas_call(
        functools.partial(back_kernel, parts, tiles),
        out_shape=(
            jax.ShapeDtypeStruct((own, local, channels), BF16),
            jax.ShapeDtypeStruct((2, share, 3 * channels), F32),
            jax.ShapeDtypeStruct((2, share, channels), F32),
        ),
        in_specs=[VMEM] * 3,
        out_specs=(VMEM,) * 3,
        scratch_shapes=[
            pltpu.VMEM((parts + 2 * MAXOFF, rows, channels), BF16),
            pltpu.VMEM((4, chips, 2 * share, channels), BF16),
            pltpu.VMEM((4, chips, 2 * share, channels), BF16),
            pltpu.VMEM((parts, chips, 2 * share, channels), BF16),
            pltpu.VMEM((chips, 2 * share, channels), BF16),
            pltpu.VMEM((chips, 2 * share, channels), BF16),
            pltpu.VMEM((2 * share, channels), BF16),
            pltpu.VMEM((parts, 2 * share, channels), BF16),
            pltpu.VMEM((8, 128), F32),
            pltpu.VMEM((tiles, 8, 128), F32),
            dma(parts), dma(parts), dma(1), dma(parts), dma(chips), dma(parts), dma(tiles),
        ],
        compiler_params=pltpu.CompilerParams(
            collective_id=1, has_side_effects=True, vmem_limit_bytes=40 * 2**20
        ),
    )(dx, raw, turn)


def body(feats, types, valid, offsets, w_qkv, w_out, d_out):
    own, row_count, col_count, channels = feats.shape
    parts = lax.axis_size("agent")
    tiles = lax.axis_size("tile")
    assert row_count == parts == 4
    local = row_count * col_count
    offs = lax.dynamic_slice_in_dim(offsets, lax.axis_index("agent") * own, own, 0)
    gone = -(1 << 20)
    rows_in = row_count + 2 * MAXOFF
    col = jnp.arange(col_count)[:, None]
    agent = jnp.arange(own)[None, :]
    from_col = col + offs[None, :, 1]
    warp = agent * (rows_in * col_count) + (MAXOFF + offs[None, :, 0]) * col_count + from_col
    warp = jnp.where((from_col >= 0) & (from_col < col_count), warp, gone).reshape(-1, 1).astype(jnp.int32)
    turn = (agent * local + col).reshape(-1, 1).astype(jnp.int32)
    x, g = front(
        feats.reshape(own, local, channels), d_out.reshape(own, local, channels), warp, turn, parts, tiles
    )
    dx, raw = layer(x, g, types, valid, w_qkv, w_out, own, tiles)
    agent = jnp.arange(own)[:, None, None]
    to_row = jnp.arange(row_count)[None, :, None] + MAXOFF - offs[:, 0][:, None, None]
    to_col = jnp.arange(col_count)[None, None, :] - offs[:, 1][:, None, None]
    home = to_row * (col_count * own) + to_col * own + agent
    home = jnp.where((to_col >= 0) & (to_col < col_count), home, gone).reshape(-1, 1).astype(jnp.int32)
    d_feats, g_qkv, g_out = back(dx, raw, home, own, tiles)
    return (d_feats.reshape(feats.shape), g_qkv, g_out)


def solution(mesh):
    placed = (
        P("agent", "tile", None, None),
        P(),
        P(),
        P(),
        P(),
        P(),
        P("agent", "tile", None, None),
    )
    return jax.shard_map(
        body,
        mesh=mesh,
        in_specs=placed,
        out_specs=(P("agent", "tile", None, None), P(None, "tile", None), P(None, "tile", None)),
        check_vma=False,
    )
```

time: 160 us -> 66.8 us (0.42)
  blocking collectives: 48.4 us -> 0 us
  Pallas kernels: 11.5 us -> 57.9 us
  starting transfers between devices: 34.6 us -> 0 us
  between operations: 32 us -> 0.73 us
  waiting for transfers between devices: 18.9 us -> 0 us
  local copies, waits for them, and re-layouts: 10.8 us -> 7.56 us
  other arithmetic: 2.71 us -> 0.33 us
    pallas_call x1 -> x3, Pallas kernels: 11.5 us -> 57.9 us  [the longest x1 32.4 us: back(): pl.pallas_call(functools.partial(back_kernel, parts, tiles), out_shape=(j...]
    unnamed x1 -> x0, blocking collectives: 38.9 us -> none
    all_to_all x6 -> x0, starting transfers between devices: 28.2 us -> none  [the longest x1 8.83 us: body(): lax.all_to_all(part, 'tile', 0, 0, axis_index_groups=lines, tiled=True)]
    all_to_all x6 -> x0, waiting for transfers between devices: 18.9 us -> none  [the longest x1 7.18 us: body(): lax.all_to_all(warped, 'agent', split_axis=0, concat_axis=1, tiled=True)]
    all_gather x1 -> x0, blocking collectives: 9.45 us -> none  [body(): whole = lax.all_gather(part, 'agent')]
    ppermute x4 -> x0, starting transfers between devices: 6.39 us -> none  [the longest x2 3.8 us: with_halo(): lax.ppermute(tail, 'tile', [(i, i + 1) for i in range(ends)])]
    unnamed x33 -> x17, local copies, waits for them, and re-layouts: 2.03 us -> 6.97 us
    slice x7 -> x0, local copies, waits for them, and re-layouts: 3.33 us -> none  [the longest x2 1.32 us: body(): return (d_feats, whole[..., :3 * channels], whole[..., 3 * channels:])]
  transfers between devices with their start and end apart: 10 -> 0, of which waited for: 4 -> 0; matrix products, arithmetic and copies ran while one was open for 5% -> 0% of each run, Pallas kernels for 0% -> 0%
where the time goes in v2:
time: 66.8 us; the launch traced here: 66.6 us
  Pallas kernels  57.9 us (87%)
  local copies, waits for them, and re-layouts  7.56 us (11%)
  between operations  0.73 us (1%)
    pallas_call x1, Pallas kernels, back(): pl.pallas_call(functools.partial(back_kernel, parts, tiles), out_shape=(j...  32.4 us
    pallas_call x1, Pallas kernels, front(): pl.pallas_call(functools.partial(front_kernel, parts, tiles), out_shape=(...  14 us
    pallas_call x1, Pallas kernels, layer(): pl.pallas_call(functools.partial(layer_kernel, agents, cells, own, tiles)...  11.5 us
    unnamed x17, local copies, waits for them, and re-layouts  6.97 us

profile of v2, /device:TPU:0, one launch (start us, length us, event | category | flops | bytes accessed | tf_op | source)
XLA Modules:
  0.0 66.6 jit_solution(10238124887680716243)
XLA Ops:
  0.6 0.0 copy-start
  0.6 0.7 copy-done
  1.3 0.1 constant_dynamic-slice_fusion
  1.4 0.1 select_n.36.warp_ref
  1.5 0.1 add.145.turn_ref
  1.6 0.0 copy-start.1
  1.6 1.0 %copy-done.1 = bf16[8,4,24,256]{3,2,1,0:T(8,128)(2,1)S(1)} copy-done((bf16[8,4,24,256]{3,2,1,0:T(8,128)(2,1)S(1)}, bf16[8,4,24,256]{3,2,1,0:T(8,128)(2,1)}, u32[]{:S(2)}) %copy-start.1) | copy-done | bytes 393240
  2.6 1.0 %copy-done.2 = bf16[8,4,24,256]{3,2,1,0:T(8,128)(2,1)S(1)} copy-done((bf16[8,4,24,256]{3,2,1,0:T(8,128)(2,1)S(1)}, bf16[8,4,24,256]{3,2,1,0:T(8,128)(2,1)}, u32[]{:S(2)}) %copy-start.2) | copy-done | bytes 393240
  3.6 14.0 %shard_map.94 = (bf16[768,256]{1,0:T(8,128)(2,1)S(1)}, bf16[768,256]{1,0:T(8,128)(2,1)S(1)}) custom-call(bf16[8,96,256]{2,1,0:T(8,128)(2,1)S(1)} %bitcast.12, bf16[8,96,256]{2,1,0:T(8,128)(2,1)S(1)} %bitcast.13, s32[192,1]{1,0:T(8,128)S(1)} %select_n.36.warp_ref, s32[192,1]{1,0:T(8,128)S(1)} %add.145.turn_ref), custom_call_target="tpu_custom_call" | custom-call | tf_op jit(solution)/shard_map/pallas_call | solution.py:238
  17.6 0.6 copy-done.5
  18.3 0.1 copy.14.types_ref
  18.4 0.7 copy-done.6
  19.0 0.1 copy.15.valid_ref
  19.1 0.9 %copy-done.4 = bf16[2,256,256]{2,1,0:T(8,128)(2,1)S(1)} copy-done((bf16[2,256,256]{2,1,0:T(8,128)(2,1)S(1)}, bf16[2,256,256]{2,1,0:T(8,128)(2,1)}, u32[]{:S(2)}) %copy-start.4) | copy-done | bytes 262168
  20.1 11.5 %shard_map.95 = (bf16[4,192,256]{2,1,0:T(8,128)(2,1)S(1)}, bf16[2,4,4,64,256]{4,3,2,1,0:T(8,128)(2,1)S(1)}) custom-call(bf16[768,256]{1,0:T(8,128)(2,1)S(1)} %get-tuple-element.10.x_ref, bf16[768,256]{1,0:T(8,128)(2,1)S(1)} %get-tuple-element.11.g_ref, s32[32,1]{1,0:T(8,128)S(1)} %copy.14.types_ref, s32[32,1]{1,0:T(8,128)S(1)} %copy.15.valid_ref, ...), custom_call_target="tpu_custom_call" | custom-call | flops 8000000000 | bytes 5000000 | tf_op jit(solution)/shard_map/pallas_call | solution.py:124
  31.6 0.1 fusion.3
  31.7 0.1 fusion.6
  31.8 0.1 subtract_multiply_fusion
  31.8 0.1 add_select_fusion
  31.9 0.2 select_n.37.turn_ref
  32.1 32.4 %shard_map.96 = (bf16[8,96,256]{2,1,0:T(8,128)(2,1)S(1)}, f32[2,32,768]{2,1,0:T(8,128)S(1)}, f32[2,32,256]{2,1,0:T(8,128)S(1)}) custom-call(bf16[4,192,256]{2,1,0:T(8,128)(2,1)S(1)} %get-tuple-element.12.dx_ref, bf16[2,4,4,64,256]{4,3,2,1,0:T(8,128)(2,1)S(1)} %get-tuple-element.13.raw_ref, s32[768,1]{1,0:T(8,128)S(1)} %select_n.37.turn_ref), custom_call_target="tpu_custom_call" | custom-call | tf_op jit(solution)/shard_map/pallas_call | solution.py:380
  64.5 0.7 %copy.20 = bf16[8,4,24,256]{3,2,1,0:T(8,128)(2,1)} copy(bf16[8,4,24,256]{3,2,1,0:T(8,128)(2,1)S(1)} %bitcast.11) | data formatting | bytes 786432
  65.3 0.7 %copy.21 = f32[2,32,768]{2,1,0:T(8,128)} copy(f32[2,32,768]{2,1,0:T(8,128)S(1)} %get-tuple-element.23) | data formatting | bytes 393216
  65.9 0.6 copy.22
  (12 shorter events, 0.0 us)
Async XLA Ops:
  0.6 0.7 %copy-start = (s32[32,2]{0,1:T(2,128)S(1)}, s32[32,2]{0,1:T(2,128)}, u32[]{:S(2)}) copy-start(s32[32,2]{0,1:T(2,128)} %param.10) | copy-start | bytes 772
  1.6 1.0 %copy-start.1 = (bf16[8,4,24,256]{3,2,1,0:T(8,128)(2,1)S(1)}, bf16[8,4,24,256]{3,2,1,0:T(8,128)(2,1)}, u32[]{:S(2)}) copy-start(bf16[8,4,24,256]{3,2,1,0:T(8,128)(2,1)} %param.7) | copy-start | bytes 1179652
  2.6 1.0 %copy-start.2 = (bf16[8,4,24,256]{3,2,1,0:T(8,128)(2,1)S(1)}, bf16[8,4,24,256]{3,2,1,0:T(8,128)(2,1)}, u32[]{:S(2)}) copy-start(bf16[8,4,24,256]{3,2,1,0:T(8,128)(2,1)} %param.13) | copy-start | bytes 1179652
  3.6 15.5 %copy-start.3 = (bf16[2,256,768]{2,1,0:T(8,128)(2,1)S(1)}, bf16[2,256,768]{2,1,0:T(8,128)(2,1)}, u32[]{:S(2)}) copy-start(bf16[2,256,768]{2,1,0:T(8,128)(2,1)} %wqkv_ref.1) | copy-start | bytes 2359300
  17.6 0.7 copy-start.5
  18.4 0.7 copy-start.6
  19.1 1.0 %copy-start.4 = (bf16[2,256,256]{2,1,0:T(8,128)(2,1)S(1)}, bf16[2,256,256]{2,1,0:T(8,128)(2,1)}, u32[]{:S(2)}) copy-start(bf16[2,256,256]{2,1,0:T(8,128)(2,1)} %wout_ref.1) | copy-start | bytes 786436

commit v3 on v1

v3 whole, which is shorter than its diff:
```python
import functools
import math

import jax
import jax.numpy as jnp
from jax import lax
from jax.experimental import pallas as pl
from jax.experimental.pallas import tpu as pltpu
from jax.sharding import PartitionSpec as P

HEADS = 8
MAXOFF = 2
F32 = jnp.float32
BF16 = jnp.bfloat16


def dot(a, b, ca, cb):
    return lax.dot_general(a, b, (((ca,), (cb,)), ((), ())), preferred_element_type=F32)


VMEM = pl.BlockSpec(memory_space=pltpu.VMEM)
HBM = pl.BlockSpec(memory_space=pltpu.HBM)
SMEM = pl.BlockSpec(memory_space=pltpu.SMEM)
MESH = pl.DeviceIdType.MESH
GONE = -(1 << 20)


def one_hot(target, width):
    lanes = lax.broadcasted_iota(jnp.int32, (target.shape[0], width), 1)
    return jnp.where(lanes == target, 1.0, 0.0).astype(BF16)


def greet(others):
    barrier = pltpu.get_barrier_semaphore()
    for there, device in others:
        @pl.when(there)
        def _(device=device):
            pl.semaphore_signal(barrier, inc=1, device_id=device, device_id_type=MESH)
    count = sum(jnp.where(there, 1, 0) for there, _ in others)
    pl.semaphore_wait(barrier, count)


def sender(src, dst, sems, k, device):
    return pltpu.make_async_remote_copy(
        src_ref=src, dst_ref=dst, send_sem=sems.at[0, k], recv_sem=sems.at[1, k], device_id=device, device_id_type=MESH
    )


def spelled(index, values):
    out = jnp.zeros_like(index)
    for j, value in enumerate(values):
        out = jnp.where(index == j, value, out)
    return out


def kernel(parts, tiles, agents, feats_ref, types_ref, valid_ref, offs_ref, wqkv_hbm, wout_hbm, grads_hbm,
           df_ref, gq_ref, go_ref,
           rim, grads, wqkv_ref, wout_ref, x_send, g_send, x_recv, g_recv, x_ref, g_ref,
           qkv_s, da_s, att_s, dqkv_s, head_s, dx, raw, back_rim, pair, first, agent_in, second, line_in,
           final, every, square, squares,
           load_sem, halo_sem, x_sem, g_sem, dx_sem, side_sem, pair_sem, agent_sem, line_sem, every_sem, square_sem):
    me, tile = lax.axis_index("agent"), lax.axis_index("tile")
    core, chip = lax.rem(tile, 2), tile // 2
    chips = tiles // 2
    own, local, channels = feats_ref.shape
    cells = local // parts
    edge = MAXOFF * cells
    inner = rim.shape[1]
    left, right = tile > 0, tile < tiles - 1
    always = parts > 0
    peers = [lax.rem(me + k, parts) for k in range(parts)]

    loads = [
        pltpu.make_async_copy(grads_hbm, grads, load_sem.at[0]),
        pltpu.make_async_copy(feats_ref, rim.at[:, edge:inner - edge, :], load_sem.at[1]),
        pltpu.make_async_copy(wout_hbm, wout_ref, load_sem.at[2]),
        pltpu.make_async_copy(wqkv_hbm, wqkv_ref, load_sem.at[3]),
    ]
    for copy in loads:
        copy.start()
    greet(
        [(always, (peers[k], tile)) for k in range(1, parts)]
        + [(always, (me, lax.rem(tile + k, tiles))) for k in range(1, tiles)]
    )
    to_right = sender(feats_ref.at[:, local - edge:, :], rim.at[:, :edge, :], halo_sem, 0, (me, tile + 1))
    to_left = sender(feats_ref.at[:, :edge, :], rim.at[:, inner - edge:, :], halo_sem, 1, (me, tile - 1))

    @pl.when(right)
    def _():
        to_right.start()

    @pl.when(left)
    def _():
        to_left.start()

    rows = cells * own

    @pl.when(tile == 0)
    def _():
        rim[:, :edge, :] = jnp.zeros((own, edge, channels), BF16)
        back_rim[:MAXOFF] = jnp.zeros((MAXOFF, rows, channels), BF16)

    @pl.when(tile == tiles - 1)
    def _():
        rim[:, inner - edge:, :] = jnp.zeros((own, edge, channels), BF16)
        back_rim[parts + MAXOFF:] = jnp.zeros((MAXOFF, rows, channels), BF16)

    def spread(source, target, send, recv, sems):
        copies = []
        for k in (*range(1, parts), 0):
            pick = one_hot(target + peers[k] * cells, source.shape[0])
            value = dot(pick, source, 1, 0).astype(BF16)
            if k == 0:
                recv[me] = value
            else:
                send[k] = value
                copies.append(sender(send.at[k], recv.at[me], sems, k, (peers[k], tile)))
                copies[-1].start()
        return copies

    def gather(copies, recv, out):
        for copy in copies:
            copy.wait()
        pieces = [recv[n].astype(F32).reshape(cells, own, channels) for n in range(parts)]
        out[...] = jnp.concatenate(pieces, axis=1).reshape(rows * parts, channels).astype(BF16)

    place = lax.broadcasted_iota(jnp.int32, (rows, 1), 0)
    whose, cell = place % own, place // own
    row_off = [offs_ref[me * own + j, 0] for j in range(own)]
    col_off = [offs_ref[me * own + j, 1] for j in range(own)]
    from_col = cell + spelled(whose, col_off)
    warp = whose * inner + (MAXOFF + spelled(whose, row_off)) * cells + from_col
    warp = jnp.where((from_col >= 0) & (from_col < cells), warp, GONE)

    loads[0].wait()
    g_copies = spread(grads[...].reshape(own * local, channels), whose * local + cell, g_send, g_recv, g_sem)
    loads[1].wait()

    @pl.when(left)
    def _():
        to_right.wait_recv()
        to_left.wait_send()

    @pl.when(right)
    def _():
        to_left.wait_recv()
        to_right.wait_send()

    x_copies = spread(rim[...].reshape(own * inner, channels), warp, x_send, x_recv, x_sem)

    size = channels // HEADS
    scale = size ** (-0.5)
    wide = HEADS * agents
    group = 8
    span = group * agents
    agent_col = lax.broadcasted_iota(jnp.int32, (agents, 1), 0)
    kind = spelled(agent_col, [types_ref[j] for j in range(agents)])
    valid = spelled(agent_col, [valid_ref[j] for j in range(agents)])
    type_wide = jnp.broadcast_to(kind, (agents, channels)).astype(F32)
    type_rows = jnp.concatenate([type_wide] * group, axis=0)
    owner = lax.broadcasted_iota(jnp.int32, (wide, channels), 0) // agents
    lane = lax.broadcasted_iota(jnp.int32, (wide, channels), 1) // size
    head_s[...] = jnp.where(owner == lane, 1.0, 0.0).astype(BF16)

    loads[2].wait()
    loads[3].wait()
    gather(g_copies, g_recv, g_ref)

    def project_g(i, _):
        at = pl.ds(pl.multiple_of(i * span, span), span)
        g = g_ref[at, :]
        a = dot(g, wout_ref[0], 1, 1)
        b = dot(g, wout_ref[1], 1, 1)
        da_s[at, :] = jnp.where(type_rows > 0.5, b, a).astype(BF16)
        return 0

    lax.fori_loop(0, cells // group, project_g, 0)
    gather(x_copies, x_recv, x_ref)

    def project(i, _):
        at = pl.ds(pl.multiple_of(i * span, span), span)
        x = x_ref[at, :]
        for j in range(3):
            cols = slice(j * channels, (j + 1) * channels)
            a = dot(x, wqkv_ref[0, :, cols], 1, 0)
            b = dot(x, wqkv_ref[1, :, cols], 1, 0)
            qkv_s[at, cols] = jnp.where(type_rows > 0.5, b, a).astype(BF16)
        return 0

    lax.fori_loop(0, cells // group, project, 0)

    key_id = lax.broadcasted_iota(jnp.int32, (agents, wide), 0)
    query_id = lax.broadcasted_iota(jnp.int32, (agents, wide), 1) % agents
    allowed = (jnp.broadcast_to(valid, (agents, wide)) == 1) | (key_id == query_id)
    lane_head = lax.broadcasted_iota(jnp.int32, (agents, channels), 1) // size

    def own_heads(full):
        out = full[:agents]
        for h in range(1, HEADS):
            out = jnp.where(lane_head == h, full[h * agents:(h + 1) * agents], out)
        return out

    def attend(i, _):
        at = pl.ds(pl.multiple_of(i * agents, agents), agents)
        q = qkv_s[at, :channels]
        k = qkv_s[at, channels:2 * channels]
        v = qkv_s[at, 2 * channels:]
        da = da_s[at, :]
        mask = head_s[...]
        qx = jnp.concatenate([q] * HEADS, axis=0) * mask
        dax = jnp.concatenate([da] * HEADS, axis=0) * mask
        scores = dot(k, qx, 1, 1) * scale
        raised = jnp.where(allowed, jnp.exp(scores), 0.0)
        prob = raised / jnp.sum(raised, axis=0, keepdims=True)
        low = prob.astype(BF16)
        pg = dot(v, dax, 1, 1)
        sg = (prob * (pg - jnp.sum(prob * pg, axis=0, keepdims=True)) * scale).astype(BF16)
        dqkv_s[at, channels:2 * channels] = dot(sg, qx, 1, 0).astype(BF16)
        dqkv_s[at, 2 * channels:] = dot(low, dax, 1, 0).astype(BF16)
        att_s[at, :] = own_heads(dot(low, v, 0, 0)).astype(BF16)
        dqkv_s[at, :channels] = own_heads(dot(sg, k, 0, 0)).astype(BF16)
        return 0

    lax.fori_loop(0, cells, attend, 0, unroll=4)

    share = channels // tiles
    ones = jnp.concatenate([type_wide.astype(BF16)] * cells, axis=0)
    for t in range(2):
        pick = ones if t else (1 - ones).astype(BF16)
        xt = x_ref[...] * pick
        for j in range(4):
            if j < 3:
                full = dot(xt, dqkv_s[:, j * channels:(j + 1) * channels], 0, 0)
            else:
                full = dot(att_s[...] * pick, g_ref[...], 0, 0)
            for i in range(tiles):
                raw[i % 2, j, i // 2, t * share:(t + 1) * share, :] = full[i * share:(i + 1) * share].astype(BF16)
    swap = sender(raw.at[1 - core], pair, pair_sem, 0, (me, tile + 1 - 2 * core))
    swap.start()

    def back(i, _):
        at = pl.ds(pl.multiple_of(i * span, span), span)
        d = dqkv_s[at, :]
        a = dot(d, wqkv_ref[0], 1, 1)
        b = dot(d, wqkv_ref[1], 1, 1)
        full = jnp.where(type_rows > 0.5, b, a).reshape(group, agents, channels)
        for n in range(parts):
            part = full[:, n * own:(n + 1) * own].reshape(group * own, channels)
            dx[n, pl.ds(pl.multiple_of(i * group * own, group * own), group * own), :] = part.astype(BF16)
        return 0

    lax.fori_loop(0, cells // group, back, 0)
    homes = [sender(dx.at[peers[k]], back_rim.at[me + MAXOFF], dx_sem, k, (peers[k], tile)) for k in range(1, parts)]
    for copy in homes:
        copy.start()
    back_rim[me + MAXOFF] = dx[me]

    swap.wait()
    first[...] = (raw[core].astype(F32) + pair[...].astype(F32)).astype(BF16)
    agent_copies = [sender(first.at[peers[k]], agent_in.at[k], agent_sem, k, (peers[k], tile)) for k in range(1, parts)]
    for copy in agent_copies:
        copy.start()

    for copy in homes:
        copy.wait()
    side_left = sender(
        back_rim.at[MAXOFF:2 * MAXOFF], back_rim.at[parts + MAXOFF:], side_sem, 0, (me, tile - 1)
    )
    side_right = sender(back_rim.at[parts:parts + MAXOFF], back_rim.at[:MAXOFF], side_sem, 1, (me, tile + 1))

    @pl.when(left)
    def _():
        side_left.start()

    @pl.when(right)
    def _():
        side_right.start()

    for copy in agent_copies:
        copy.wait()
    total = first[me].astype(F32)
    for k in range(1, parts):
        total = total + agent_in[k].astype(F32)
    second[...] = total.astype(BF16)
    line_copies = []
    for k in range(1, chips):
        other = lax.rem(chip + k, chips)
        line_copies.append(sender(second.at[other], line_in.at[k], line_sem, k, (me, 2 * other + core)))
        line_copies[-1].start()

    @pl.when(left)
    def _():
        side_right.wait_recv()
        side_left.wait_send()

    @pl.when(right)
    def _():
        side_left.wait_recv()
        side_right.wait_send()

    def restore(agent_ids):
        source = back_rim[...].reshape(back_rim.shape[0] * rows, channels)
        spot = lax.broadcasted_iota(jnp.int32, (local, 1), 0)
        for i in agent_ids:
            col = spot % cells - col_off[i]
            home = (spot // cells + MAXOFF - row_off[i]) * rows + col * own + i
            pick = one_hot(jnp.where((col >= 0) & (col < cells), home, GONE), source.shape[0])
            df_ref[i] = dot(pick, source, 1, 0).astype(BF16)

    restore(range(own // 2))
    for copy in line_copies:
        copy.wait()
    total = second[chip].astype(F32)
    for k in range(1, chips):
        total = total + line_in[k].astype(F32)
    final[...] = total.astype(BF16)
    every[me] = total.astype(BF16)
    every_copies = [sender(final, every.at[me], every_sem, k, (peers[k], tile)) for k in range(1, parts)]
    for copy in every_copies:
        copy.start()
    restore(range(own // 2, own - 1))
    for copy in every_copies:
        copy.wait()
    whole = every[...].astype(F32)
    summed = jnp.sum(whole * whole, axis=0)
    summed = jnp.sum(jnp.sum(summed, axis=0, keepdims=True), axis=1, keepdims=True)
    level = jnp.broadcast_to(summed, (8, 128))
    square[...] = level
    squares[tile] = level
    square_copies = [
        sender(square, squares.at[tile], square_sem, k, (me, lax.rem(tile + k, tiles))) for k in range(1, tiles)
    ]
    for copy in square_copies:
        copy.start()
    restore(range(own - 1, own))
    for copy in square_copies:
        copy.wait()
    norm = jnp.sqrt(jnp.sum(squares[...], axis=0)[:1, :1])
    limit = math.sqrt(8.0 * channels * channels)
    factor = limit / jnp.maximum(norm, limit)
    for t in range(2):
        for j in range(4):
            piece = every[j].astype(F32)[t * share:(t + 1) * share] * factor
            if j < 3:
                gq_ref[t, :, j * channels:(j + 1) * channels] = piece
            else:
                go_ref[t] = piece


def body(feats, types, valid, offsets, w_qkv, w_out, d_out):
    own, row_count, cells, channels = feats.shape
    parts = lax.axis_size("agent")
    tiles = lax.axis_size("tile")
    assert row_count == parts == 4
    agents = own * parts
    local = row_count * cells
    inner = local + 2 * MAXOFF * cells
    rows = cells * own
    n = cells * agents
    chips = tiles // 2
    share = channels // tiles
    block = pltpu.VMEM((parts, rows, channels), BF16)
    pieces = pltpu.VMEM((4, chips, 2 * share, channels), BF16)
    line = pltpu.VMEM((chips, 2 * share, channels), BF16)

    def dma(count):
        return pltpu.SemaphoreType.DMA((2, count))

    d_feats, g_qkv, g_out = pl.pallas_call(
        functools.partial(kernel, parts, tiles, agents),
        out_shape=(
            jax.ShapeDtypeStruct((own, local, channels), BF16),
            jax.ShapeDtypeStruct((2, share, 3 * channels), F32),
            jax.ShapeDtypeStruct((2, share, channels), F32),
        ),
        in_specs=[HBM, SMEM, SMEM, SMEM, HBM, HBM, HBM],
        out_specs=(VMEM,) * 3,
        scratch_shapes=[
            pltpu.VMEM((own, inner, channels), BF16),
            pltpu.VMEM((own, local, channels), BF16),
            pltpu.VMEM(w_qkv.shape, BF16),
            pltpu.VMEM(w_out.shape, BF16),
            block, block, block, block,
            pltpu.VMEM((n, channels), BF16),
            pltpu.VMEM((n, channels), BF16),
            pltpu.VMEM((n, 3 * channels), BF16),
            pltpu.VMEM((n, channels), BF16),
            pltpu.VMEM((n, channels), BF16),
            pltpu.VMEM((n, 3 * channels), BF16),
            pltpu.VMEM((HEADS * agents, channels), BF16),
            block,
            pltpu.VMEM((2, 4, chips, 2 * share, channels), BF16),
            pltpu.VMEM((parts + 2 * MAXOFF, rows, channels), BF16),
            pieces, pieces,
            pltpu.VMEM((parts, chips, 2 * share, channels), BF16),
            line, line,
            pltpu.VMEM((2 * share, channels), BF16),
            pltpu.VMEM((parts, 2 * share, channels), BF16),
            pltpu.VMEM((8, 128), F32),
            pltpu.VMEM((tiles, 8, 128), F32),
            pltpu.SemaphoreType.DMA((4,)),
            dma(2), dma(parts), dma(parts), dma(parts), dma(2), dma(1), dma(parts), dma(chips), dma(parts), dma(tiles),
        ],
        compiler_params=pltpu.CompilerParams(
            collective_id=0, has_side_effects=True, vmem_limit_bytes=48 * 2**20
        ),
    )(feats.reshape(own, local, channels), types, valid, offsets, w_qkv, w_out, d_out.reshape(own, local, channels))
    return (d_feats.reshape(feats.shape), g_qkv, g_out)


def solution(mesh):
    placed = (
        P("agent", "tile", None, None),
        P(),
        P(),
        P(),
        P(),
        P(),
        P("agent", "tile", None, None),
    )
    return jax.shard_map(
        body,
        mesh=mesh,
        in_specs=placed,
        out_specs=(P("agent", "tile", None, None), P(None, "tile", None), P(None, "tile", None)),
        check_vma=False,
    )
```

time: 160 us -> 62.4 us (0.39)
  blocking collectives: 48.4 us -> 0 us
  Pallas kernels: 11.5 us -> 54 us
  starting transfers between devices: 34.6 us -> 0 us
  between operations: 32 us -> 0.66 us
  waiting for transfers between devices: 18.9 us -> 0 us
  local copies, waits for them, and re-layouts: 10.8 us -> 7.47 us
  other arithmetic: 2.71 us -> 0 us
    pallas_call x1, Pallas kernels: 11.5 us -> 54 us  [body(): pl.pallas_call(functools.partial(kernel, parts, tiles, agents), out_shape...]
    unnamed x1 -> x0, blocking collectives: 38.9 us -> none
    all_to_all x6 -> x0, starting transfers between devices: 28.2 us -> none  [the longest x1 8.83 us: body(): lax.all_to_all(part, 'tile', 0, 0, axis_index_groups=lines, tiled=True)]
    all_to_all x6 -> x0, waiting for transfers between devices: 18.9 us -> none  [the longest x1 7.18 us: body(): lax.all_to_all(warped, 'agent', split_axis=0, concat_axis=1, tiled=True)]
    all_gather x1 -> x0, blocking collectives: 9.45 us -> none  [body(): whole = lax.all_gather(part, 'agent')]
    ppermute x4 -> x0, starting transfers between devices: 6.39 us -> none  [the longest x2 3.8 us: with_halo(): lax.ppermute(tail, 'tile', [(i, i + 1) for i in range(ends)])]
    unnamed x33 -> x18, local copies, waits for them, and re-layouts: 2.03 us -> 7.47 us
    slice x7 -> x0, local copies, waits for them, and re-layouts: 3.33 us -> none  [the longest x2 1.32 us: body(): return (d_feats, whole[..., :3 * channels], whole[..., 3 * channels:])]
  transfers between devices with their start and end apart: 10 -> 0, of which waited for: 4 -> 0; matrix products, arithmetic and copies ran while one was open for 5% -> 0% of each run, Pallas kernels for 0% -> 0%
where the time goes in v3:
time: 62.4 us; the launch traced here: 62.1 us
  Pallas kernels  54 us (87%)
  local copies, waits for them, and re-layouts  7.47 us (12%)
  between operations  0.66 us (1%)
    pallas_call x1, Pallas kernels, body(): pl.pallas_call(functools.partial(kernel, parts, tiles, agents), out_shape...  54 us
    unnamed x18, local copies, waits for them, and re-layouts  7.47 us

profile of v3, /device:TPU:0, one launch (start us, length us, event | category | flops | bytes accessed | tf_op | source)
XLA Modules:
  0.0 62.1 jit_solution(531655476377230433)
XLA Ops:
  0.6 0.0 copy-start.6
  0.6 0.7 %copy-done.6 = s32[32,2]{0,1:T(2,128)S(1)} copy-done((s32[32,2]{0,1:T(2,128)S(1)}, s32[32,2]{0,1:T(2,128)}, u32[]{:S(2)}) %copy-start.6) | copy-done | bytes 280
  1.3 0.0 copy-start.4
  1.3 0.0 copy-start.5
  1.3 0.1 copy.10.offs_ref
  1.4 0.6 copy-done.4
  2.0 0.0 copy-done.5
  2.0 0.0 copy-start
  2.0 1.1 %copy-done = bf16[2,256,768]{2,1,0:T(8,128)(2,1)S(1)} copy-done((bf16[2,256,768]{2,1,0:T(8,128)(2,1)S(1)}, bf16[2,256,768]{2,1,0:T(8,128)(2,1)}, u32[]{:S(2)}) %copy-start) | copy-done | bytes 786456
  3.1 0.0 copy-start.1
  3.1 1.0 %copy-done.1 = bf16[8,4,24,256]{3,2,1,0:T(8,128)(2,1)S(1)} copy-done((bf16[8,4,24,256]{3,2,1,0:T(8,128)(2,1)S(1)}, bf16[8,4,24,256]{3,2,1,0:T(8,128)(2,1)}, u32[]{:S(2)}) %copy-start.1) | copy-done | bytes 393240
  4.1 0.0 copy-start.2
  4.1 1.0 %copy-done.2 = bf16[8,4,24,256]{3,2,1,0:T(8,128)(2,1)S(1)} copy-done((bf16[8,4,24,256]{3,2,1,0:T(8,128)(2,1)S(1)}, bf16[8,4,24,256]{3,2,1,0:T(8,128)(2,1)}, u32[]{:S(2)}) %copy-start.2) | copy-done | bytes 393240
  5.1 0.0 copy-start.3
  5.1 0.9 %copy-done.3 = bf16[2,256,256]{2,1,0:T(8,128)(2,1)S(1)} copy-done((bf16[2,256,256]{2,1,0:T(8,128)(2,1)S(1)}, bf16[2,256,256]{2,1,0:T(8,128)(2,1)}, u32[]{:S(2)}) %copy-start.3) | copy-done | bytes 262168
  6.1 54.0 %shard_map.94 = (bf16[8,96,256]{2,1,0:T(8,128)(2,1)S(1)}, f32[2,32,768]{2,1,0:T(8,128)S(1)}, f32[2,32,256]{2,1,0:T(8,128)S(1)}) custom-call(bf16[8,96,256]{2,1,0:T(8,128)(2,1)S(1)} %bitcast.4, s32[32]{0:T(128)S(1)} %copy-done.4, s32[32]{0:T(128)S(1)} %copy-done.5, s32[32,2]{1,0:T(8,128)S(1)} %copy.10.offs_ref, bf16[2,256,768]{2,1,0:T(8,128)(2,1)S(1)} %copy-done, ...), custom_call_target="tpu_custom_call" | custom-call | tf_op jit(solution)/shard_map/pallas_call | solution.py:369
  60.0 0.7 %copy.14 = bf16[8,4,24,256]{3,2,1,0:T(8,128)(2,1)} copy(bf16[8,4,24,256]{3,2,1,0:T(8,128)(2,1)S(1)} %bitcast.3) | data formatting | bytes 786432
  60.8 0.7 %copy.15 = f32[2,32,768]{2,1,0:T(8,128)} copy(f32[2,32,768]{2,1,0:T(8,128)S(1)} %get-tuple-element.13) | data formatting | bytes 393216
  61.5 0.6 %copy.16 = f32[2,32,256]{2,1,0:T(8,128)} copy(f32[2,32,256]{2,1,0:T(8,128)S(1)} %get-tuple-element.14) | data formatting | bytes 131072
Async XLA Ops:
  0.6 0.7 %copy-start.6 = (s32[32,2]{0,1:T(2,128)S(1)}, s32[32,2]{0,1:T(2,128)}, u32[]{:S(2)}) copy-start(s32[32,2]{0,1:T(2,128)} %param.10) | copy-start | bytes 772
  1.3 0.7 %copy-start.4 = (s32[32]{0:T(128)S(1)}, s32[32]{0:T(128)}, u32[]{:S(2)}) copy-start(s32[32]{0:T(128)} %types_ref.1) | copy-start | bytes 388
  1.3 0.7 %copy-start.5 = (s32[32]{0:T(128)S(1)}, s32[32]{0:T(128)}, u32[]{:S(2)}) copy-start(s32[32]{0:T(128)} %valid_ref.1) | copy-start | bytes 388
  2.0 1.1 %copy-start = (bf16[2,256,768]{2,1,0:T(8,128)(2,1)S(1)}, bf16[2,256,768]{2,1,0:T(8,128)(2,1)}, u32[]{:S(2)}) copy-start(bf16[2,256,768]{2,1,0:T(8,128)(2,1)} %wqkv_hbm.1) | copy-start | bytes 2359300
  3.1 1.0 %copy-start.1 = (bf16[8,4,24,256]{3,2,1,0:T(8,128)(2,1)S(1)}, bf16[8,4,24,256]{3,2,1,0:T(8,128)(2,1)}, u32[]{:S(2)}) copy-start(bf16[8,4,24,256]{3,2,1,0:T(8,128)(2,1)} %param.7) | copy-start | bytes 1179652
  4.1 1.0 %copy-start.2 = (bf16[8,4,24,256]{3,2,1,0:T(8,128)(2,1)S(1)}, bf16[8,4,24,256]{3,2,1,0:T(8,128)(2,1)}, u32[]{:S(2)}) copy-start(bf16[8,4,24,256]{3,2,1,0:T(8,128)(2,1)} %param.13) | copy-start | bytes 1179652
  5.1 0.9 %copy-start.3 = (bf16[2,256,256]{2,1,0:T(8,128)(2,1)S(1)}, bf16[2,256,256]{2,1,0:T(8,128)(2,1)}, u32[]{:S(2)}) copy-start(bf16[2,256,256]{2,1,0:T(8,128)(2,1)} %wout_hbm.1) | copy-start | bytes 786436

commit v4 on v3

--- a/solution.py
+++ b/solution.py
@@ -55,8 +55,8 @@
 
 def kernel(parts, tiles, agents, feats_ref, types_ref, valid_ref, offs_ref, wqkv_hbm, wout_hbm, grads_hbm,
            df_ref, gq_ref, go_ref,
-           rim, grads, wqkv_ref, wout_ref, x_send, g_send, x_recv, g_recv, x_ref, g_ref,
-           qkv_s, da_s, att_s, dqkv_s, head_s, dx, raw, back_rim, pair, first, agent_in, second, line_in,
+           rim, grads, warped, wqkv_ref, wout_ref, x_send, g_send, x_recv, g_recv, x_ref, g_ref,
+           qkv_s, da_s, att_s, dqkv_s, head_s, dx, dx_send, raw, back_rim, pair, first, agent_in, second, line_in,
            final, every, square, squares,
            load_sem, halo_sem, x_sem, g_sem, dx_sem, side_sem, pair_sem, agent_sem, line_sem, every_sem, square_sem):
     me, tile = lax.axis_index("agent"), lax.axis_index("tile")
@@ -98,18 +98,30 @@
     @pl.when(tile == 0)
     def _():
         rim[:, :edge, :] = jnp.zeros((own, edge, channels), BF16)
-        back_rim[:MAXOFF] = jnp.zeros((MAXOFF, rows, channels), BF16)
+        back_rim[:MAXOFF] = jnp.zeros((MAXOFF, own, cells, channels), BF16)
 
     @pl.when(tile == tiles - 1)
     def _():
         rim[:, inner - edge:, :] = jnp.zeros((own, edge, channels), BF16)
-        back_rim[parts + MAXOFF:] = jnp.zeros((MAXOFF, rows, channels), BF16)
-
-    def spread(source, target, send, recv, sems):
+        back_rim[parts + MAXOFF:] = jnp.zeros((MAXOFF, own, cells, channels), BF16)
+
+    place = lax.broadcasted_iota(jnp.int32, (rows, 1), 0)
+    to_cells = one_hot((place % own) * cells + place // own, rows)
+    to_agents = one_hot((place % cells) * own + place // cells, rows)
+    spot = lax.broadcasted_iota(jnp.int32, (local, 1), 0)
+    row_off = [offs_ref[me * own + j, 0] for j in range(own)]
+    col_off = [offs_ref[me * own + j, 1] for j in range(own)]
+
+    def shift(i, direction):
+        col = spot % cells + direction * col_off[i]
+        target = (spot // cells + MAXOFF + direction * row_off[i]) * cells + col
+        return one_hot(jnp.where((col >= 0) & (col < cells), target, GONE), inner)
+
+    def spread(source, send, recv, sems):
         copies = []
         for k in (*range(1, parts), 0):
-            pick = one_hot(target + peers[k] * cells, source.shape[0])
-            value = dot(pick, source, 1, 0).astype(BF16)
+            part = source[:, peers[k]].astype(F32).reshape(rows, channels).astype(BF16)
+            value = dot(to_cells, part, 1, 0).astype(BF16)
             if k == 0:
                 recv[me] = value
             else:
@@ -124,16 +136,8 @@
         pieces = [recv[n].astype(F32).reshape(cells, own, channels) for n in range(parts)]
         out[...] = jnp.concatenate(pieces, axis=1).reshape(rows * parts, channels).astype(BF16)
 
-    place = lax.broadcasted_iota(jnp.int32, (rows, 1), 0)
-    whose, cell = place % own, place // own
-    row_off = [offs_ref[me * own + j, 0] for j in range(own)]
-    col_off = [offs_ref[me * own + j, 1] for j in range(own)]
-    from_col = cell + spelled(whose, col_off)
-    warp = whose * inner + (MAXOFF + spelled(whose, row_off)) * cells + from_col
-    warp = jnp.where((from_col >= 0) & (from_col < cells), warp, GONE)
-
     loads[0].wait()
-    g_copies = spread(grads[...].reshape(own * local, channels), whose * local + cell, g_send, g_recv, g_sem)
+    g_copies = spread(grads, g_send, g_recv, g_sem)
     loads[1].wait()
 
     @pl.when(left)
@@ -146,7 +150,9 @@
         to_left.wait_recv()
         to_right.wait_send()
 
-    x_copies = spread(rim[...].reshape(own * inner, channels), warp, x_send, x_recv, x_sem)
+    for i in range(own):
+        warped[i] = dot(shift(i, 1), rim[i], 1, 0).reshape(parts, cells, channels)
+    x_copies = spread(warped, x_send, x_recv, x_sem)
 
     size = channels // HEADS
     scale = size ** (-0.5)
@@ -250,10 +256,15 @@
         return 0
 
     lax.fori_loop(0, cells // group, back, 0)
-    homes = [sender(dx.at[peers[k]], back_rim.at[me + MAXOFF], dx_sem, k, (peers[k], tile)) for k in range(1, parts)]
-    for copy in homes:
-        copy.start()
-    back_rim[me + MAXOFF] = dx[me]
+    homes = []
+    for k in (*range(1, parts), 0):
+        value = dot(to_agents, dx[peers[k]], 1, 0).reshape(own, cells, channels).astype(BF16)
+        if k == 0:
+            back_rim[me + MAXOFF] = value
+        else:
+            dx_send[k] = value
+            homes.append(sender(dx_send.at[k], back_rim.at[me + MAXOFF], dx_sem, k, (peers[k], tile)))
+            homes[-1].start()
 
     swap.wait()
     first[...] = (raw[core].astype(F32) + pair[...].astype(F32)).astype(BF16)
@@ -299,13 +310,9 @@
         side_right.wait_send()
 
     def restore(agent_ids):
-        source = back_rim[...].reshape(back_rim.shape[0] * rows, channels)
-        spot = lax.broadcasted_iota(jnp.int32, (local, 1), 0)
         for i in agent_ids:
-            col = spot % cells - col_off[i]
-            home = (spot // cells + MAXOFF - row_off[i]) * rows + col * own + i
-            pick = one_hot(jnp.where((col >= 0) & (col < cells), home, GONE), source.shape[0])
-            df_ref[i] = dot(pick, source, 1, 0).astype(BF16)
+            source = back_rim[:, i].astype(F32).reshape(inner, channels).astype(BF16)
+            df_ref[i] = dot(shift(i, -1), source, 1, 0).astype(BF16)
 
     restore(range(own // 2))
     for copy in line_copies:
@@ -377,7 +384,8 @@
         out_specs=(VMEM,) * 3,
         scratch_shapes=[
             pltpu.VMEM((own, inner, channels), BF16),
-            pltpu.VMEM((own, local, channels), BF16),
+            pltpu.VMEM((own, parts, cells, channels), BF16),
+            pltpu.VMEM((own, parts, cells, channels), F32),
             pltpu.VMEM(w_qkv.shape, BF16),
             pltpu.VMEM(w_out.shape, BF16),
             block, block, block, block,
@@ -389,8 +397,9 @@
             pltpu.VMEM((n, 3 * channels), BF16),
             pltpu.VMEM((HEADS * agents, channels), BF16),
             block,
+            pltpu.VMEM((parts, own, cells, channels), BF16),
             pltpu.VMEM((2, 4, chips, 2 * share, channels), BF16),
-            pltpu.VMEM((parts + 2 * MAXOFF, rows, channels), BF16),
+            pltpu.VMEM((parts + 2 * MAXOFF, own, cells, channels), BF16),
             pieces, pieces,
             pltpu.VMEM((parts, chips, 2 * share, channels), BF16),
             line, line,
@@ -404,7 +413,7 @@
         compiler_params=pltpu.CompilerParams(
             collective_id=0, has_side_effects=True, vmem_limit_bytes=48 * 2**20
         ),
-    )(feats.reshape(own, local, channels), types, valid, offsets, w_qkv, w_out, d_out.reshape(own, local, channels))
+    )(feats.reshape(own, local, channels), types, valid, offsets, w_qkv, w_out, d_out)
     return (d_feats.reshape(feats.shape), g_qkv, g_out)
 
 

time: 62.4 us -> 62.5 us (level)
  no operation moved by 1% of the time
where the time goes in v4:
time: 62.5 us; the launch traced here: 62.2 us
  Pallas kernels  54.1 us (87%)
  local copies, waits for them, and re-layouts  7.47 us (12%)
  between operations  0.66 us (1%)
    pallas_call x1, Pallas kernels, body(): pl.pallas_call(functools.partial(kernel, parts, tiles, agents), out_shape...  54.1 us
    unnamed x18, local copies, waits for them, and re-layouts  7.47 us

profile of v4, /device:TPU:0, one launch (start us, length us, event | category | flops | bytes accessed | tf_op | source)
XLA Modules:
  0.0 62.2 jit_solution(4534288794490944829)
XLA Ops:
  0.6 0.0 copy-start.6
  0.6 0.7 %copy-done.6 = s32[32,2]{0,1:T(2,128)S(1)} copy-done((s32[32,2]{0,1:T(2,128)S(1)}, s32[32,2]{0,1:T(2,128)}, u32[]{:S(2)}) %copy-start.6) | copy-done | bytes 280
  1.3 0.0 copy-start.4
  1.3 0.0 copy-start.5
  1.3 0.1 copy.10.offs_ref
  1.4 0.6 copy-done.4
  2.0 0.0 copy-done.5
  2.0 0.0 copy-start
  2.0 1.1 %copy-done = bf16[2,256,768]{2,1,0:T(8,128)(2,1)S(1)} copy-done((bf16[2,256,768]{2,1,0:T(8,128)(2,1)S(1)}, bf16[2,256,768]{2,1,0:T(8,128)(2,1)}, u32[]{:S(2)}) %copy-start) | copy-done | bytes 786456
  3.1 0.0 copy-start.1
  3.1 1.0 %copy-done.1 = bf16[8,4,24,256]{3,2,1,0:T(8,128)(2,1)S(1)} copy-done((bf16[8,4,24,256]{3,2,1,0:T(8,128)(2,1)S(1)}, bf16[8,4,24,256]{3,2,1,0:T(8,128)(2,1)}, u32[]{:S(2)}) %copy-start.1) | copy-done | bytes 393240
  4.1 0.0 copy-start.2
  4.1 1.0 %copy-done.2 = bf16[8,4,24,256]{3,2,1,0:T(8,128)(2,1)S(1)} copy-done((bf16[8,4,24,256]{3,2,1,0:T(8,128)(2,1)S(1)}, bf16[8,4,24,256]{3,2,1,0:T(8,128)(2,1)}, u32[]{:S(2)}) %copy-start.2) | copy-done | bytes 393240
  5.1 0.0 copy-start.3
  5.1 0.9 %copy-done.3 = bf16[2,256,256]{2,1,0:T(8,128)(2,1)S(1)} copy-done((bf16[2,256,256]{2,1,0:T(8,128)(2,1)S(1)}, bf16[2,256,256]{2,1,0:T(8,128)(2,1)}, u32[]{:S(2)}) %copy-start.3) | copy-done | bytes 262168
  6.1 54.1 %shard_map.94 = (bf16[8,96,256]{2,1,0:T(8,128)(2,1)S(1)}, f32[2,32,768]{2,1,0:T(8,128)S(1)}, f32[2,32,256]{2,1,0:T(8,128)S(1)}) custom-call(bf16[8,96,256]{2,1,0:T(8,128)(2,1)S(1)} %bitcast.3, s32[32]{0:T(128)S(1)} %copy-done.4, s32[32]{0:T(128)S(1)} %copy-done.5, s32[32,2]{1,0:T(8,128)S(1)} %copy.10.offs_ref, bf16[2,256,768]{2,1,0:T(8,128)(2,1)S(1)} %copy-done, ...), custom_call_target="tpu_custom_call" | custom-call | tf_op jit(solution)/shard_map/pallas_call | solution.py:376
  60.2 0.7 %copy.14 = bf16[8,4,24,256]{3,2,1,0:T(8,128)(2,1)} copy(bf16[8,4,24,256]{3,2,1,0:T(8,128)(2,1)S(1)} %bitcast.2) | data formatting | bytes 786432
  60.9 0.7 %copy.15 = f32[2,32,768]{2,1,0:T(8,128)} copy(f32[2,32,768]{2,1,0:T(8,128)S(1)} %get-tuple-element.13) | data formatting | bytes 393216
  61.6 0.6 %copy.16 = f32[2,32,256]{2,1,0:T(8,128)} copy(f32[2,32,256]{2,1,0:T(8,128)S(1)} %get-tuple-element.14) | data formatting | bytes 131072
Async XLA Ops:
  0.6 0.7 %copy-start.6 = (s32[32,2]{0,1:T(2,128)S(1)}, s32[32,2]{0,1:T(2,128)}, u32[]{:S(2)}) copy-start(s32[32,2]{0,1:T(2,128)} %param.10) | copy-start | bytes 772
  1.3 0.7 %copy-start.4 = (s32[32]{0:T(128)S(1)}, s32[32]{0:T(128)}, u32[]{:S(2)}) copy-start(s32[32]{0:T(128)} %types_ref.1) | copy-start | bytes 388
  1.3 0.7 %copy-start.5 = (s32[32]{0:T(128)S(1)}, s32[32]{0:T(128)}, u32[]{:S(2)}) copy-start(s32[32]{0:T(128)} %valid_ref.1) | copy-start | bytes 388
  2.0 1.1 %copy-start = (bf16[2,256,768]{2,1,0:T(8,128)(2,1)S(1)}, bf16[2,256,768]{2,1,0:T(8,128)(2,1)}, u32[]{:S(2)}) copy-start(bf16[2,256,768]{2,1,0:T(8,128)(2,1)} %wqkv_hbm.1) | copy-start | bytes 2359300
  3.1 1.0 %copy-start.1 = (bf16[8,4,24,256]{3,2,1,0:T(8,128)(2,1)S(1)}, bf16[8,4,24,256]{3,2,1,0:T(8,128)(2,1)}, u32[]{:S(2)}) copy-start(bf16[8,4,24,256]{3,2,1,0:T(8,128)(2,1)} %param.7) | copy-start | bytes 1179652
  4.1 1.0 %copy-start.2 = (bf16[8,4,24,256]{3,2,1,0:T(8,128)(2,1)S(1)}, bf16[8,4,24,256]{3,2,1,0:T(8,128)(2,1)}, u32[]{:S(2)}) copy-start(bf16[8,4,24,256]{3,2,1,0:T(8,128)(2,1)} %grads_hbm.1) | copy-start | bytes 1179652
  5.1 0.9 %copy-start.3 = (bf16[2,256,256]{2,1,0:T(8,128)(2,1)S(1)}, bf16[2,256,256]{2,1,0:T(8,128)(2,1)}, u32[]{:S(2)}) copy-start(bf16[2,256,256]{2,1,0:T(8,128)(2,1)} %wout_hbm.1) | copy-start | bytes 786436

commit v5 on v4

--- a/solution.py
+++ b/solution.py
@@ -411,7 +411,7 @@
             dma(2), dma(parts), dma(parts), dma(parts), dma(2), dma(1), dma(parts), dma(chips), dma(parts), dma(tiles),
         ],
         compiler_params=pltpu.CompilerParams(
-            collective_id=0, has_side_effects=True, vmem_limit_bytes=48 * 2**20
+            collective_id=0, has_side_effects=True, vmem_limit_bytes=63 * 2**20
         ),
     )(feats.reshape(own, local, channels), types, valid, offsets, w_qkv, w_out, d_out)
     return (d_feats.reshape(feats.shape), g_qkv, g_out)

time: 62.5 us -> 60.3 us (0.965)
  local copies, waits for them, and re-layouts: 7.47 us -> 4.66 us
    unnamed x18 -> x10, local copies, waits for them, and re-layouts: 7.47 us -> 4.66 us
    pallas_call x1, Pallas kernels: 54.1 us -> 54.7 us  [body(): pl.pallas_call(functools.partial(kernel, parts, tiles, agents), out_shape...]
where the time goes in v5:
time: 60.3 us; the launch traced here: 60 us
  Pallas kernels  54.7 us (91%)
  local copies, waits for them, and re-layouts  4.66 us (8%)
  between operations  0.66 us (1%)
    pallas_call x1, Pallas kernels, body(): pl.pallas_call(functools.partial(kernel, parts, tiles, agents), out_shape...  54.7 us
    unnamed x10, local copies, waits for them, and re-layouts  4.66 us

profile of v5, /device:TPU:0, one launch (start us, length us, event | category | flops | bytes accessed | tf_op | source)
XLA Modules:
  0.0 60.0 jit_solution(672332249254178438)
XLA Ops:
  0.6 0.0 copy-start.2
  0.6 0.7 %copy-done.2 = s32[32,2]{0,1:T(2,128)S(1)} copy-done((s32[32,2]{0,1:T(2,128)S(1)}, s32[32,2]{0,1:T(2,128)}, u32[]{:S(2)}) %copy-start.2) | copy-done | bytes 280
  1.3 0.7 %copy.10.offs_ref = s32[32,2]{1,0:T(8,128)} copy(s32[32,2]{0,1:T(2,128)S(1)} %copy-done.2) | data formatting | bytes 512 | tf_op args[3]
  2.0 54.7 %shard_map.94 = (bf16[8,96,256]{2,1,0:T(8,128)(2,1)}, f32[2,32,768]{2,1,0:T(8,128)}, f32[2,32,256]{2,1,0:T(8,128)}) custom-call(bf16[8,96,256]{2,1,0:T(8,128)(2,1)} %bitcast.3, s32[32]{0:T(128)} %types_ref.1, s32[32]{0:T(128)} %valid_ref.1, s32[32,2]{1,0:T(8,128)} %copy.10.offs_ref, bf16[2,256,768]{2,1,0:T(8,128)(2,1)} %wqkv_hbm.1, ...), custom_call_target="tpu_custom_call" | custom-call | tf_op jit(solution)/shard_map/pallas_call | solution.py:376
  56.7 0.0 copy-start
  56.7 1.8 %copy.14 = bf16[8,4,24,256]{3,2,1,0:T(8,128)(2,1)} copy(bf16[8,4,24,256]{3,2,1,0:T(8,128)(2,1)} %bitcast.2) | data formatting | bytes 786432
  58.6 0.0 copy-done
  58.6 0.0 copy-start.1
  58.6 0.7 %copy.15 = f32[2,32,768]{2,1,0:T(8,128)} copy(f32[2,32,768]{2,1,0:T(8,128)S(1)} %copy-done) | data formatting | bytes 393216
  59.2 0.2 copy-done.1
  59.4 0.6 %copy.16 = f32[2,32,256]{2,1,0:T(8,128)} copy(f32[2,32,256]{2,1,0:T(8,128)S(1)} %copy-done.1) | data formatting | bytes 131072
Async XLA Ops:
  0.6 0.7 %copy-start.2 = (s32[32,2]{0,1:T(2,128)S(1)}, s32[32,2]{0,1:T(2,128)}, u32[]{:S(2)}) copy-start(s32[32,2]{0,1:T(2,128)} %param.10) | copy-start | bytes 772
  56.7 1.8 %copy-start = (f32[2,32,768]{2,1,0:T(8,128)S(1)}, f32[2,32,768]{2,1,0:T(8,128)}, u32[]{:S(2)}) copy-start(f32[2,32,768]{2,1,0:T(8,128)} %get-tuple-element.13) | copy-start | bytes 589828
  58.6 0.9 %copy-start.1 = (f32[2,32,256]{2,1,0:T(8,128)S(1)}, f32[2,32,256]{2,1,0:T(8,128)}, u32[]{:S(2)}) copy-start(f32[2,32,256]{2,1,0:T(8,128)} %get-tuple-element.14) | copy-start | bytes 196612
